TPU v7x, 32 devices: a whole 2x2x4 slice. The times are simulated.
32 devices in a mesh: gx: 8 (over z, y), gy: 4 (over x, core).
Axes of the slice: x: 2, y: 2, z: 4, core: 2. Of those that a mesh axis runs over, the one named last changes fastest.
Arguments:
- flux_perturbation: float32 [2, 4096, 4096], P(None, 'gx', 'gy'), may hold values from -6 to 6
- archived_nominal_heat_levels: float32 [2, 2, 4096, 4096], P(None, None, 'gx', 'gy'), may hold values from -4 to 4
- archived_solidity_labels: int32 [2, 2, 4096, 4096], P(None, None, 'gx', 'gy'), may hold values from 0 to 2
Outputs:
- hess_vec: float32 [2, 4096, 4096], P(None, 'gx', 'gy')
Inputs may be any that keep to these rules, and one draw needn't show every extreme that they name: `archived_solidity_labels`: 0 is solid, 1 mushy, 2 liquid.
All inputs are finite; a program needn't handle non-finite values.
Results may differ from a plain program's by a relative error of at most 0.000061.
Values sent between devices are 32-bit elements; how exact they have to be, the bound alone decides.
A program may use at most 192 MiB of HBM per device.

v0:
```python
import math

import jax
import jax.numpy as jnp
from jax import lax
from jax.sharding import PartitionSpec as P

TIME_STEP = 0.1
OBS_WEIGHT = 10.0
PRIOR_GAIN = 0.005
HIGHEST = lax.Precision.HIGHEST


def with_halo(cells, sides, width):
    for axis, dim in sides:
        count = lax.axis_size(axis)
        ends = count - 1
        head = lax.slice_in_dim(cells, 0, width, axis=dim)
        tail = lax.slice_in_dim(cells, cells.shape[dim] - width, cells.shape[dim], axis=dim)
        cells = jnp.concatenate(
            [
                lax.ppermute(tail, axis, [(i, (i + 1) % count) for i in range(ends)]),
                cells,
                lax.ppermute(head, axis, [((i + 1) % count, i) for i in range(ends)]),
            ],
            axis=dim,
        )
    return cells


def surface_rim(field):
    padded = with_halo(field, (("gx", 1), ("gy", 2)), 1)
    return padded[:, 2:, 1:-1] + padded[:, :-2, 1:-1] + padded[:, 1:-1, 2:] + padded[:, 1:-1, :-2]


def cos_sin(horizontal_line_total, col_count, modulus):
    row_ids = jnp.arange(horizontal_line_total, dtype=jnp.int32)[:, None]
    col_ids = jnp.arange(col_count, dtype=jnp.int32)[None, :]
    angles = (row_ids * col_ids % modulus).astype(jnp.float32) * (2.0 * math.pi / modulus)
    return (jnp.cos(angles), jnp.sin(angles))


def tables(length):
    bit_count = length.bit_length() - 1
    outer_len = 2 ** (bit_count // 2)
    inner_len = length // outer_len
    cos_outer, sin_outer = cos_sin(outer_len, outer_len, outer_len)
    cos_inner, sin_inner = cos_sin(inner_len, inner_len, inner_len)
    twist_cos, twist_sin = cos_sin(outer_len, inner_len, length)
    outer_fwd = jnp.stack([cos_outer, -sin_outer])
    inner_fwd = jnp.stack([jnp.stack([cos_inner, -sin_inner]), jnp.stack([sin_inner, cos_inner])])
    inner_inv = jnp.stack([jnp.stack([cos_inner, sin_inner]), jnp.stack([-sin_inner, cos_inner])])
    outer_inv = jnp.stack([cos_outer, -sin_outer])
    freq_index = (
        jnp.arange(outer_len, dtype=jnp.int32)[:, None]
        + outer_len * jnp.arange(inner_len, dtype=jnp.int32)[None, :]
    )
    signed = jnp.where(freq_index < length // 2, freq_index, freq_index - length).astype(
        jnp.float32
    )
    wave_sq = (signed * (2.0 * math.pi / length)) ** 2
    return (
        length,
        outer_len,
        inner_len,
        outer_fwd,
        inner_fwd,
        inner_inv,
        outer_inv,
        twist_cos,
        twist_sin,
        wave_sq,
    )


def forward(field, table):
    (
        length,
        outer_len,
        inner_len,
        outer_fwd,
        inner_fwd,
        inner_inv,
        outer_inv,
        twist_cos,
        twist_sin,
        wave_sq,
    ) = table
    grid = field.reshape(field.shape[:-1] + (outer_len, inner_len))
    stepped = jnp.einsum("...ab,rak->...rkb", grid, outer_fwd, precision=HIGHEST)
    step_re = stepped[..., 0, :, :]
    step_im = stepped[..., 1, :, :]
    twisted = jnp.stack(
        [step_re * twist_cos + step_im * twist_sin, step_im * twist_cos - step_re * twist_sin],
        axis=-3,
    )
    spec = jnp.einsum("...rkb,rsbm->...skm", twisted, inner_fwd, precision=HIGHEST)
    return (spec[..., 0, :, :], spec[..., 1, :, :])


def inverse(spec_re, spec_im, table):
    (
        length,
        outer_len,
        inner_len,
        outer_fwd,
        inner_fwd,
        inner_inv,
        outer_inv,
        twist_cos,
        twist_sin,
        wave_sq,
    ) = table
    stacked = jnp.stack([spec_re, spec_im], axis=-3)
    halved = jnp.einsum("...skm,srbm->...rkb", stacked, inner_inv, precision=HIGHEST)
    half_re = halved[..., 0, :, :]
    half_im = halved[..., 1, :, :]
    turned = jnp.stack(
        [half_re * twist_cos - half_im * twist_sin, half_im * twist_cos + half_re * twist_sin],
        axis=-3,
    )
    grid = jnp.einsum("...rkb,rka->...ab", turned, outer_inv, precision=HIGHEST)
    return grid.reshape(grid.shape[:-2] + (length,)) / length


def shards(flux_perturbation, archived_nominal_heat_levels, archived_solidity_labels):
    capacity = jnp.where(
        archived_solidity_labels == 0, 1.0, jnp.where(archived_solidity_labels == 1, 4.0, 1.25)
    ).astype(jnp.float32)
    diffusion_advance = jnp.where(
        archived_solidity_labels == 0, 1.0, jnp.where(archived_solidity_labels == 1, 0.6, 0.35)
    ).astype(jnp.float32)
    diffusion_advance = diffusion_advance * (1.0 + 0.5 * jnp.tanh(archived_nominal_heat_levels))
    rows = lax.all_to_all(flux_perturbation, "gx", split_axis=2, concat_axis=1, tiled=True)
    row_table = tables(rows.shape[1])
    first_u = TIME_STEP * flux_perturbation / capacity[0, 0]
    second_top = TIME_STEP * flux_perturbation + TIME_STEP * (
        diffusion_advance[0, 0] * (surface_rim(first_u) - 6.0 * first_u) + flux_perturbation
    )
    second_low = TIME_STEP * diffusion_advance[0, 1] * first_u
    top_u = second_top / capacity[1, 0]
    low_u = second_low / capacity[1, 1]
    third_top = second_top + TIME_STEP * (
        diffusion_advance[1, 0] * (surface_rim(top_u) - 6.0 * top_u + low_u) + flux_perturbation
    )
    misfit = OBS_WEIGHT * third_top / capacity[1, 0]
    adj_three = misfit / capacity[1, 0]
    push_top = TIME_STEP * diffusion_advance[1, 0] * adj_three
    adj_two_top = adj_three + (surface_rim(push_top) - 6.0 * push_top) / capacity[1, 0]
    adj_two_low = push_top / capacity[1, 1]
    pull_top = TIME_STEP * diffusion_advance[0, 0] * adj_two_top
    pull_low = TIME_STEP * diffusion_advance[0, 1] * adj_two_low
    adj_one_top = adj_two_top + (surface_rim(pull_top) - 6.0 * pull_top + pull_low) / capacity[0, 0]
    data_term = TIME_STEP * (adj_three + adj_two_top + adj_one_top)
    row_re, row_im = forward(jnp.swapaxes(rows, 1, 2), row_table)
    wave_x = row_table[-1]
    second_x = jnp.swapaxes(
        inverse(2.0 * PRIOR_GAIN * wave_x * row_re, 2.0 * PRIOR_GAIN * wave_x * row_im, row_table),
        1,
        2,
    )
    fourth_x = jnp.swapaxes(
        inverse(
            PRIOR_GAIN * wave_x * wave_x * row_re, PRIOR_GAIN * wave_x * wave_x * row_im, row_table
        ),
        1,
        2,
    )
    second_back, fourth_part = (
        lax.all_to_all(second_x, "gx", split_axis=1, concat_axis=2, tiled=True),
        lax.all_to_all(fourth_x, "gx", split_axis=1, concat_axis=2, tiled=True),
    )
    cols_dir, cols_second = (
        lax.all_to_all(flux_perturbation, "gy", split_axis=1, concat_axis=2, tiled=True),
        lax.all_to_all(second_back, "gy", split_axis=1, concat_axis=2, tiled=True),
    )
    col_table = tables(cols_dir.shape[2])
    dir_re, dir_im = forward(cols_dir, col_table)
    sec_re, sec_im = forward(cols_second, col_table)
    wave_y = col_table[-1]
    mixed = inverse(
        PRIOR_GAIN * wave_y * wave_y * dir_re + wave_y * sec_re,
        PRIOR_GAIN * wave_y * wave_y * dir_im + wave_y * sec_im,
        col_table,
    )
    mixed_back = lax.all_to_all(mixed, "gy", split_axis=2, concat_axis=1, tiled=True)
    return data_term + fourth_part + mixed_back


def solution(mesh):
    in_specs = (P(None, "gx", "gy"), P(None, None, "gx", "gy"), P(None, None, "gx", "gy"))
    out_specs = P(None, "gx", "gy")
    return jax.shard_map(shards, mesh=mesh, in_specs=in_specs, out_specs=out_specs, check_vma=False)
```

profile of v0, /device:TPU:17, one launch (start us, length us, event | category | flops | bytes accessed | tf_op | source)
XLA Modules:
  0.0 816.4 jit_solution(504303709747888213)
XLA Ops:
  0.0 7.4 copy.232
  7.4 5.5 all-to-all-start.2
  12.9 7.2 copy.218
  20.1 40.2 %all-to-all-done.2 = f32[2,512,1024]{2,0,1:T(2,128)} async-done(((f32[2,512,1024]{2,0,1:T(2,128)}), f32[2,512,1024]{2,0,1:T(2,128)}, u32[]{:S(2)}, u32[]{:S(2)}) %all-to-all-start.2) | async-done | bytes 4194336 | tf_op jit(solution)/shard_map/all_to_all | solution.py:174
  60.3 5.8 all-to-all-start
  67.5 5.6 copy.233
  73.1 5.3 copy.234
  78.5 13.3 %fusion.81 = f32[2,128,2,64,64]{1,3,4,0,2:T(8,128)} fusion(f32[2,128,64,64]{1,3,2,0:T(8,128)} %bitcast.223, f32[1,64,64]{1,2,0:T(8,128)S(1)} %get-tuple-element.69, f32[1,64,64]{1,2,0:T(8,128)S(1)} %get-tuple-element.70), kind=kOutput, calls=%fused_computation.149 | convolution fusion | flops 1610620928 | bytes 12615680 | tf_op jit(solution)/shard_map/...ab,rak->...rkb/dot_general | solution.py:90
  91.8 63.4 %all-to-all-done = f32[2,512,1024]{1,0,2:T(2,128)} async-done(((f32[2,512,1024]{1,0,2:T(2,128)}), f32[2,512,1024]{1,0,2:T(2,128)}, u32[]{:S(2)}, u32[]{:S(2)}) %all-to-all-start) | async-done | bytes 4194336 | tf_op jit(solution)/shard_map/all_to_all | solution.py:134
  155.2 5.0 copy.219
  160.2 5.4 copy.220
  165.6 11.7 %fusion.78 = f32[2,128,2,64,64]{1,3,4,0,2:T(8,128)S(1)} fusion(f32[2,128,64,64]{1,3,2,0:T(8,128)} %bitcast.224, f32[1,64,64]{1,2,0:T(8,128)S(1)} %get-tuple-element.69, f32[1,64,64]{1,2,0:T(8,128)S(1)} %get-tuple-element.70), kind=kOutput, calls=%fused_computation.148 | convolution fusion | flops 1610620928 | bytes 12615680 | tf_op jit(solution)/shard_map/...ab,rak->...rkb/dot_general | solution.py:90
  180.5 12.5 %fusion.87 = f32[2,128,2,64,64]{1,4,3,0,2:T(8,128)S(1)} fusion(f32[2,128,2,64,64]{1,3,4,0,2:T(8,128)S(1)} %pad_maximum_fusion, f32[1,2,64,64]{2,3,1,0:T(8,128)S(1)} %get-tuple-element.61, f32[1,2,64,64]{2,3,1,0:T(8,128)S(1)} %get-tuple-element.64), kind=kOutput, calls=%fused_computation.151 | convolution fusion | flops 3221241856 | bytes 16842752 | tf_op jit(solution)/shard_map/...rkb,rsbm->...skm/dot_general | solution.py:97
  193.1 3.5 slice_multiply_fusion.7
  196.6 8.5 %fusion.90 = f32[2,64,2,128,64]{3,1,4,2,0:T(8,128)S(1)} fusion(f32[2,128,1,64,64]{1,4,3,0,2:T(8,128)S(1)} %get-tuple-element.27, f32[2,128,1,64,64]{1,4,3,0,2:T(8,128)S(1)} %get-tuple-element.26, f32[1,2,64,64]{2,3,1,0:T(8,128)S(1)} %get-tuple-element.65, f32[1,2,64,64]{2,3,1,0:T(8,128)S(1)} %get-tuple-element.60), kind=kOutput, calls=%fused_computation.152 | convolution fusion | flops 3223339008 | bytes 16842752 | tf_op jit(solution)/shard_map/...skm,srbm->...rkb/dot_general | solution.py:115
  205.1 8.4 %copy.364 = f32[2,64,2,128,64]{3,4,1,2,0:T(8,128)} copy(f32[2,64,2,128,64]{3,1,4,2,0:T(8,128)S(1)} %fusion.90) | data formatting | bytes 16777216 | tf_op jit(solution)/shard_map/...skm,srbm->...rkb/dot_general | solution.py:115
  213.5 10.7 %fusion.96 = f32[2,64,2,128,64]{3,1,4,2,0:T(8,128)S(1)} fusion(f32[2,128,1,64,64]{1,4,3,0,2:T(8,128)S(1)} %get-tuple-element.38, f32[2,128,1,64,64]{1,4,3,0,2:T(8,128)} %get-tuple-element.39, f32[1,2,64,64]{2,3,1,0:T(8,128)S(1)} %get-tuple-element.65, f32[1,2,64,64]{2,3,1,0:T(8,128)S(1)} %get-tuple-element.60), kind=kOutput, calls=%fused_computation.154 | convolution fusion | flops 3223339008 | bytes 16842752 | tf_op jit(solution)/shard_map/...skm,srbm->...rkb/dot_general | solution.py:115
  224.2 8.5 %copy.363 = f32[2,64,2,128,64]{3,4,1,2,0:T(8,128)} copy(f32[2,64,2,128,64]{3,1,4,2,0:T(8,128)S(1)} %fusion.96) | data formatting | bytes 16777216 | tf_op jit(solution)/shard_map/...skm,srbm->...rkb/dot_general | solution.py:115
  232.7 12.8 %multiply_subtract_fusion.4 = (f32[2,128,1,64,64]{1,3,4,0,2:T(8,128)}, f32[2,128,1,64,64]{1,3,4,0,2:T(8,128)}, f32[2,128,1,64,64]{1,3,4,0,2:T(8,128)}, f32[2,128...) fusion(f32[2,128,2,64,64]{1,3,4,0,2:T(8,128)} %bitcast.221, ...), kind=kLoop, calls=%fused_computation.138 | loop fusion | flops 18874368 | bytes 50364416 | tf_op jit(solution)/shard_map/sub | solution.py:119
  245.6 4.9 fusion.66
  252.9 16.4 %copy.245 = f32[2,4096,128]{2,0,1:T(2,128)} copy(f32[2,4096,128]{2,1,0:T(8,128)S(1)} %bitcast.228) | data formatting | bytes 8388608 | tf_op jit(solution)/shard_map/transpose | solution.py:157
  269.3 8.0 all-to-all-start.3
  277.3 5.4 copy.181
  282.7 83.3 %all-to-all-done.3 = f32[2,4096,128]{2,0,1:T(2,128)} async-done(((f32[2,4096,128]{2,0,1:T(2,128)}), f32[2,4096,128]{2,0,1:T(2,128)}, u32[]{:S(2)}, u32[]{:S(2)}) %all-to-all-start.3) | async-done | bytes 4194336 | tf_op jit(solution)/shard_map/all_to_all | solution.py:170
  366.0 4.5 copy.246
  370.5 5.4 copy.247
  375.9 7.4 copy.248
  383.3 7.3 all-to-all-start.4
  390.5 9.8 %add_multiply_fusion = (f32[2,2,512,1024]{3,2,1,0:T(8,128)}, pred[2,2,512,1024]{3,2,1,0:T(8,128)(4,1)S(1)}, pred[2,2,512,1024]{3,2,1,0:T(8,128)(4,1)S(1)}) fusion(f32[2,2,512,1024]{3,2,1,0:T(8,128)} %param.4, s32[2,2,512,1024]{3,2,1,0:T(8,128)} %param.5), kind=kLoop, calls=%fused_computation.40 | loop fusion | flops 14680064 | bytes 29360128 | tf_op jit(solution)/shard_map/mul | solution.py:133
  423.1 7.3 fusion.67
  432.8 16.2 %copy.229 = f32[2,4096,128]{2,0,1:T(2,128)} copy(f32[2,4096,128]{2,1,0:T(8,128)S(1)} %bitcast.231) | data formatting | bytes 8388608 | tf_op jit(solution)/shard_map/transpose | solution.py:162
  449.0 8.1 all-to-all-start.1
  457.1 5.8 slice_bitcast_fusion.2
  466.9 4.4 collective-permute-start.3
  473.2 5.2 broadcast_multiply_fusion.3
  484.3 14.6 %broadcast_divide_fusion = f32[2,512,1024]{1,2,0:T(8,128)S(1)} fusion(f32[512,1024]{0,1:T(8,128)} %copy.192, f32[2,512,1024]{1,2,0:T(8,128)} %copy.181, f32[2,512,1024]{1,2,0:T(8,128)} %copy-done, f32[2,1,1024]{1,2,0:T(8,128)S(1)} %copy.185, f32[2,1,1024]{1,2,0:T(8,128)} %copy.187, f32[2,514,1]{1,2,0:T(1,128)S(1)} %collective-permute-done.3, ...), kind=kLoop, calls=%fused_computation.166 | loop fusion | flops 19922944 | bytes 16801824 | tf_op jit(solution)/shard_map/div | solution.py:141
  531.5 15.3 %collective-permute-done.4 = f32[2,1,1024]{2,0,1:T(2,128)} collective-permute-done((f32[2,1,1024]{2,0,1:T(2,128)}, f32[2,1,1024]{2,0,1:T(2,128)}, u32[]{:S(2)}, u32[]{:S(2)}) %collective-permute-start.4) | collective-permute-done | bytes 8224 | tf_op jit(solution)/shard_map/ppermute | solution.py:24
  553.2 4.1 collective-permute-start.7
  559.2 3.4 pad_maximum_fusion.2
  562.7 13.1 %fusion.93 = f32[2,128,2,64,64]{1,4,3,0,2:T(8,128)} fusion(f32[2,128,2,64,64]{1,3,4,0,2:T(8,128)S(1)} %pad_maximum_fusion.2, f32[1,2,64,64]{2,3,1,0:T(8,128)S(1)} %get-tuple-element.61, f32[1,2,64,64]{2,3,1,0:T(8,128)S(1)} %get-tuple-element.64), kind=kOutput, calls=%fused_computation.153 | convolution fusion | flops 3221241856 | bytes 16842752 | tf_op jit(solution)/shard_map/...rkb,rsbm->...skm/dot_general | solution.py:97
  575.7 5.5 copy.249
  581.3 5.4 copy.250
  586.6 11.3 %fusion.84 = f32[2,128,2,64,64]{1,3,4,0,2:T(8,128)S(1)} fusion(f32[2,128,64,64]{1,3,2,0:T(8,128)} %bitcast.225, f32[1,64,64]{1,2,0:T(8,128)S(1)} %get-tuple-element.69, f32[1,64,64]{1,2,0:T(8,128)S(1)} %get-tuple-element.70), kind=kOutput, calls=%fused_computation.150 | convolution fusion | flops 1610620928 | bytes 12615680 | tf_op jit(solution)/shard_map/...ab,rak->...rkb/dot_general | solution.py:90
  599.7 4.1 pad_maximum_fusion.4
  603.8 15.9 %fusion.99 = f32[2,128,2,64,64]{1,4,3,0,2:T(8,128)S(1)} fusion(f32[2,128,2,64,64]{1,3,4,0,2:T(8,128)} %pad_maximum_fusion.4, f32[1,2,64,64]{2,3,1,0:T(8,128)S(1)} %get-tuple-element.61, f32[1,2,64,64]{2,3,1,0:T(8,128)S(1)} %get-tuple-element.64), kind=kOutput, calls=%fused_computation.155 | convolution fusion | flops 3221241856 | bytes 16842752 | tf_op jit(solution)/shard_map/...rkb,rsbm->...skm/dot_general | solution.py:97
  619.8 4.7 fusion.31
  624.6 10.8 %fusion.102 = f32[2,64,2,128,64]{3,1,4,2,0:T(8,128)S(1)} fusion(f32[2,128,1,64,64]{1,4,3,0,2:T(8,128)} %get-tuple-element.13, f32[2,128,1,64,64]{1,4,3,0,2:T(8,128)} %get-tuple-element.12, f32[1,2,64,64]{2,3,1,0:T(8,128)S(1)} %get-tuple-element.65, f32[1,2,64,64]{2,3,1,0:T(8,128)S(1)} %get-tuple-element.60), kind=kOutput, calls=%fused_computation.156 | convolution fusion | flops 3223339008 | bytes 16842752 | tf_op jit(solution)/shard_map/...skm,srbm->...rkb/dot_general | solution.py:115
  635.4 4.9 copy.362
  642.2 4.9 fusion.65
  649.5 16.1 %copy.259 = f32[2,128,4096]{1,0,2:T(2,128)} copy(f32[2,128,4096]{1,2,0:T(8,128)S(1)} %bitcast.233) | data formatting | bytes 8388608 | tf_op jit(solution)/shard_map/div | solution.py:123
  665.7 5.0 all-to-all-start.5
  670.7 30.2 %broadcast_multiply_fusion.1 = (f32[2,512,1024]{1,2,0:T(8,128)S(1)}, f32[2,512,1024]{1,2,0:T(8,128)}) fusion(f32[512,1024]{0,1:T(8,128)} %copy.203, f32[512,1024]{0,1:T(8,128)} %copy.202, f32[2,512,1024]{1,2,0:T(8,128)} %copy.181, f32[512,1024]{0,1:T(8,128)} %copy.200, f32[512,1024]{0,1:T(8,128)S(1)} %copy.183, f32[512,1024]{0,1:T(8,128)} %copy.199, ...), kind=kLoop, calls=%fused_computation.165 | loop fusion | flops 44040192 | bytes 35700800 | tf_op jit(solution)/shard_map/mul | solution.py:148
  705.9 5.1 collective-permute-start.8
  718.9 5.1 collective-permute-start.11
  728.9 15.4 %broadcast_multiply_fusion = (f32[2,512,1024]{1,2,0:T(8,128)S(1)}, f32[2,512,1024]{1,2,0:T(8,128)}) fusion(f32[512,1024]{0,1:T(8,128)} %copy.210, f32[2,512,1024]{1,2,0:T(8,128)} %get-tuple-element.8, f32[512,1024]{0,1:T(8,128)} %copy.192, f32[2,512,1024]{1,2,0:T(8,128)} %copy-done.3, f32[2,1,1024]{1,2,0:T(8,128)S(1)} %copy.205, f32[2,1,1024]{1,2,0:T(8,128)} %copy.207, ...), kind=kLoop, calls=%fused_computation.164 | loop fusion | flops 16777216 | bytes 20996128 | tf_op jit(solution)/shard_map/mul | solution.py:151
  751.5 3.4 collective-permute-start.13
  759.0 4.7 collective-permute-start.15
  765.7 4.4 copy.230
  770.1 5.6 copy.231
  775.7 4.5 copy.260
  780.2 5.4 copy.261
  785.6 5.4 copy.262
  791.0 19.8 %fusion.72 = f32[2,512,1024]{1,2,0:T(8,128)} fusion(f32[2,512,1024]{1,2,0:T(8,128)} %copy.262, f32[2,512,8,128]{1,3,2,0:T(8,128)} %copy.231, f32[2,512,1024]{1,2,0:T(8,128)} %get-tuple-element.6, f32[2,512,1024]{1,2,0:T(8,128)} %copy-done.2, f32[2,1,1024]{1,2,0:T(8,128)S(1)} %copy.212, f32[2,1,1024]{1,2,0:T(8,128)} %copy.214, ...), kind=kLoop, calls=%fused_computation.123 | loop fusion | flops 25165824 | bytes 33579040 | tf_op jit(solution)/shard_map/add | solution.py:187
  810.8 5.4 copy.263
  (109 shorter events, 121.9 us)
Async XLA Ops:
  7.4 52.9 %all-to-all-start.2 = ((f32[2,512,1024]{2,0,1:T(2,128)}), f32[2,512,1024]{2,0,1:T(2,128)}, u32[]{:S(2)}, u32[]{:S(2)}) async-start(f32[2,512,1024]{2,0,1:T(2,128)} %copy.232), calls=%async_computation.2 | async-start | bytes 8388608 | tf_op jit(solution)/shard_map/all_to_all | solution.py:174
  60.3 94.9 %all-to-all-start = ((f32[2,512,1024]{1,0,2:T(2,128)}), f32[2,512,1024]{1,0,2:T(2,128)}, u32[]{:S(2)}, u32[]{:S(2)}) async-start(f32[2,512,1024]{1,0,2:T(2,128)} %copy.218), calls=%async_computation | async-start | bytes 8388608 | tf_op jit(solution)/shard_map/all_to_all | solution.py:134
  67.0 126.1 %copy-start.6 = (f32[64,64]{1,0:T(8,128)}, f32[64,64]{1,0:T(8,128)S(1)}, u32[]{:S(2)}) copy-start(f32[64,64]{1,0:T(8,128)S(1)} %copy.217) | copy-start | bytes 49156
  205.1 27.6 %slice-start.2 = ((s8[8388608]{0:T(1024)(128)(4,1)}), s8[4194304]{0:T(1024)(128)(4,1)S(1)}, s32[]{:S(2)}) async-start(s8[8388608]{0:T(1024)(128)(4,1)} %bitcast.219), calls=%async_computation.8 | async-start | bytes 8388608
  213.5 19.3 %slice-start.3 = ((s8[8388608]{0:T(1024)(128)(4,1)}), s8[4194304]{0:T(1024)(128)(4,1)S(1)}, s32[]{:S(2)}) async-start(s8[8388608]{0:T(1024)(128)(4,1)} %bitcast.219), calls=%async_computation.9 | async-start | bytes 8388608
  269.3 96.7 %all-to-all-start.3 = ((f32[2,4096,128]{2,0,1:T(2,128)}), f32[2,4096,128]{2,0,1:T(2,128)}, u32[]{:S(2)}, u32[]{:S(2)}) async-start(f32[2,4096,128]{2,0,1:T(2,128)} %copy.245), calls=%async_computation.3 | async-start | bytes 8388608 | tf_op jit(solution)/shard_map/all_to_all | solution.py:170
  383.3 65.7 %all-to-all-start.4 = ((f32[2,512,1024]{2,0,1:T(2,128)}), f32[2,512,1024]{2,0,1:T(2,128)}, u32[]{:S(2)}, u32[]{:S(2)}) async-start(f32[2,512,1024]{2,0,1:T(2,128)} %copy.248), calls=%async_computation.4 | async-start | bytes 8388608 | tf_op jit(solution)/shard_map/all_to_all | solution.py:175
  401.9 5.1 copy-start.4
  412.0 2.0 copy-start
  416.9 46.0 %collective-permute-start = (f32[2,1,1024]{2,0,1:T(2,128)S(1)}, f32[2,1,1024]{2,0,1:T(2,128)S(1)}, u32[]{:S(2)}, u32[]{:S(2)}) collective-permute-start(f32[2,1,1024]{2,0,1:T(2,128)S(1)} %copy.184), channel_id=1, source_target_pairs={{4,0},{8,4},{12,8},{16,12},{20,16},{24,20},{28,24},{5,1},{9,5},{13... | collective-permute-start | bytes 24584 | tf_op jit(solution)/shard_map/ppermute | solution.py:24
  420.9 42.4 %collective-permute-start.1 = (f32[2,1,1024]{2,0,1:T(2,128)}, f32[2,1,1024]{2,0,1:T(2,128)}, u32[]{:S(2)}, u32[]{:S(2)}) collective-permute-start(f32[2,1,1024]{2,0,1:T(2,128)} %copy.186), channel_id=1, source_target_pairs={{0,4},{4,8},{8,12},{12,16},{16,20},{20,24},{24,28},{1,5},{5,9},{9,... | collective-permute-start | bytes 24584 | tf_op jit(solution)/shard_map/ppermute | solution.py:22
  449.0 216.7 %all-to-all-start.1 = ((f32[2,4096,128]{2,0,1:T(2,128)}), f32[2,4096,128]{2,0,1:T(2,128)}, u32[]{:S(2)}, u32[]{:S(2)}) async-start(f32[2,4096,128]{2,0,1:T(2,128)} %copy.229), calls=%async_computation.1 | async-start | bytes 8388608 | tf_op jit(solution)/shard_map/all_to_all | solution.py:171
  466.9 17.4 %collective-permute-start.3 = (f32[2,514,1]{1,2,0:T(1,128)}, f32[2,514,1]{1,2,0:T(1,128)S(1)}, u32[]{:S(2)}, u32[]{:S(2)}) collective-permute-start(f32[2,514,1]{1,2,0:T(1,128)} %get-tuple-element.47), channel_id=1, source_target_pairs={{0,1},{1,2},{2,3},{4,5},{5,6},{6,7},{8,9},{9,10},{10,11},{12,13},{... | collective-permute-start | bytes 12344 | tf_op jit(solution)/shard_map/ppermute | solution.py:22
  471.2 13.0 %collective-permute-start.2 = (f32[2,514,1]{1,2,0:T(1,128)}, f32[2,514,1]{1,2,0:T(1,128)S(1)}, u32[]{:S(2)}, u32[]{:S(2)}) collective-permute-start(f32[2,514,1]{1,2,0:T(1,128)} %get-tuple-element.46), channel_id=1, source_target_pairs={{1,0},{2,1},{3,2},{5,4},{6,5},{7,6},{9,8},{10,9},{11,10},{13,12},{... | collective-permute-start | bytes 12344 | tf_op jit(solution)/shard_map/ppermute | solution.py:24
  498.9 2.1 copy-start.1
  504.8 42.1 %collective-permute-start.4 = (f32[2,1,1024]{2,0,1:T(2,128)}, f32[2,1,1024]{2,0,1:T(2,128)}, u32[]{:S(2)}, u32[]{:S(2)}) collective-permute-start(f32[2,1,1024]{2,0,1:T(2,128)} %copy.193), channel_id=1, source_target_pairs={{4,0},{8,4},{12,8},{16,12},{20,16},{24,20},{28,24},{5,1},{9,5},{13... | collective-permute-start | bytes 24584 | tf_op jit(solution)/shard_map/ppermute | solution.py:24
  510.0 39.5 %collective-permute-start.5 = (f32[2,1,1024]{2,0,1:T(2,128)}, f32[2,1,1024]{2,0,1:T(2,128)}, u32[]{:S(2)}, u32[]{:S(2)}) collective-permute-start(f32[2,1,1024]{2,0,1:T(2,128)} %copy.195), channel_id=1, source_target_pairs={{0,4},{4,8},{8,12},{12,16},{16,20},{20,24},{24,28},{1,5},{5,9},{9,... | collective-permute-start | bytes 24584 | tf_op jit(solution)/shard_map/ppermute | solution.py:22
  551.6 7.6 copy-start.5
  553.2 117.5 %collective-permute-start.7 = (f32[2,514,1]{1,2,0:T(1,128)}, f32[2,514,1]{1,2,0:T(1,128)}, u32[]{:S(2)}, u32[]{:S(2)}) collective-permute-start(f32[2,514,1]{1,2,0:T(1,128)} %get-tuple-element.45), channel_id=1, source_target_pairs={{0,1},{1,2},{2,3},{4,5},{5,6},{6,7},{8,9},{9,10},{10,11},{12,13},{... | collective-permute-start | bytes 12344 | tf_op jit(solution)/shard_map/ppermute | solution.py:22
  557.3 113.4 %collective-permute-start.6 = (f32[2,514,1]{1,2,0:T(1,128)}, f32[2,514,1]{1,2,0:T(1,128)}, u32[]{:S(2)}, u32[]{:S(2)}) collective-permute-start(f32[2,514,1]{1,2,0:T(1,128)} %get-tuple-element.44), channel_id=1, source_target_pairs={{1,0},{2,1},{3,2},{5,4},{6,5},{7,6},{9,8},{10,9},{11,10},{13,12},{... | collective-permute-start | bytes 12344 | tf_op jit(solution)/shard_map/ppermute | solution.py:24
  599.7 20.1 %slice-start = ((s8[8388608]{0:T(1024)(128)(4,1)}), s8[4194304]{0:T(1024)(128)(4,1)S(1)}, s32[]{:S(2)}) async-start(s8[8388608]{0:T(1024)(128)(4,1)} %bitcast.216), calls=%async_computation.6 | async-start | bytes 8388608
  603.8 16.0 %slice-start.1 = ((s8[8388608]{0:T(1024)(128)(4,1)}), s8[4194304]{0:T(1024)(128)(4,1)S(1)}, s32[]{:S(2)}) async-start(s8[8388608]{0:T(1024)(128)(4,1)} %bitcast.216), calls=%async_computation.7 | async-start | bytes 8388608
  603.8 16.0 %copy-start.7 = (f32[64,64]{1,0:T(8,128)S(1)}, f32[64,64]{1,0:T(8,128)}, u32[]{:S(2)}) copy-start(f32[64,64]{1,0:T(8,128)} %copy-done.6) | copy-start | bytes 49156
  603.8 16.0 %copy-start.8 = (f32[64,64]{1,0:T(8,128)S(1)}, f32[64,64]{1,0:T(8,128)}, u32[]{:S(2)}) copy-start(f32[64,64]{1,0:T(8,128)} %copy.238) | copy-start | bytes 49156
  665.7 110.1 %all-to-all-start.5 = ((f32[2,128,4096]{1,0,2:T(2,128)}), f32[2,128,4096]{1,0,2:T(2,128)}, u32[]{:S(2)}, u32[]{:S(2)}) async-start(f32[2,128,4096]{1,0,2:T(2,128)} %copy.259), calls=%async_computation.5 | async-start | bytes 8388608 | tf_op jit(solution)/shard_map/all_to_all | solution.py:186
  700.9 2.0 copy-start.3
  705.9 7.4 collective-permute-start.8
  711.3 5.3 collective-permute-start.9
  718.9 9.9 %collective-permute-start.11 = (f32[2,514,1]{1,2,0:T(1,128)S(1)}, f32[2,514,1]{1,2,0:T(1,128)S(1)}, u32[]{:S(2)}, u32[]{:S(2)}) collective-permute-start(f32[2,514,1]{1,2,0:T(1,128)S(1)} %get-tuple-element.43), channel_id=1, source_target_pairs={{0,1},{1,2},{2,3},{4,5},{5,6},{6,7},{8,9},{9,10},{10,11},{12,13},{... | collective-permute-start | bytes 12344 | tf_op jit(solution)/shard_map/ppermute | solution.py:22
  724.0 4.9 collective-permute-start.10
  744.3 2.0 copy-start.2
  749.2 5.6 collective-permute-start.12
  751.5 5.3 collective-permute-start.13
  759.0 31.9 %collective-permute-start.15 = (f32[2,514,1]{1,2,0:T(1,128)S(1)}, f32[2,514,1]{1,2,0:T(1,128)S(1)}, u32[]{:S(2)}, u32[]{:S(2)}) collective-permute-start(f32[2,514,1]{1,2,0:T(1,128)S(1)} %get-tuple-element.41), channel_id=1, source_target_pairs={{0,1},{1,2},{2,3},{4,5},{5,6},{6,7},{8,9},{9,10},{10,11},{12,13},{... | collective-permute-start | bytes 12344 | tf_op jit(solution)/shard_map/ppermute | solution.py:22
  763.7 27.2 %collective-permute-start.14 = (f32[2,514,1]{1,2,0:T(1,128)S(1)}, f32[2,514,1]{1,2,0:T(1,128)S(1)}, u32[]{:S(2)}, u32[]{:S(2)}) collective-permute-start(f32[2,514,1]{1,2,0:T(1,128)S(1)} %get-tuple-element.40), channel_id=1, source_target_pairs={{1,0},{2,1},{3,2},{5,4},{6,5},{7,6},{9,8},{10,9},{11,10},{13,12},{... | collective-permute-start | bytes 12344 | tf_op jit(solution)/shard_map/ppermute | solution.py:24
where the time goes:
time: 823 us; the launch traced here: 816 us
  local copies, waits for them, and re-layouts  244 us (30%)
  waiting for transfers between devices  208 us (25%)
  other arithmetic  150 us (18%)
  matrix products  125 us (15%)
  starting transfers between devices  88.5 us (11%)
    all_to_all x1, waiting for transfers between devices, shards(): lax.all_to_all(second_x, 'gx', split_axis=1, concat_axis=2, tiled=True)  83.3 us
    all_to_all x1, waiting for transfers between devices, shards(): lax.all_to_all(flux_perturbation, 'gx', split_axis=2, concat_axis=1, tile...  63.4 us
    dot_general x3, matrix products, forward(): jnp.einsum('...rkb,rsbm->...skm', twisted, inner_fwd, precision=HIGHEST)  41.5 us
    all_to_all x1, waiting for transfers between devices, shards(): lax.all_to_all(flux_perturbation, 'gy', split_axis=1, concat_axis=2, tile...  40.2 us
    dot_general x3, matrix products, forward(): jnp.einsum('...ab,rak->...rkb', grid, outer_fwd, precision=HIGHEST)  36.2 us
    mul x2, other arithmetic, shards(): push_top = TIME_STEP * diffusion_advance[1, 0] * adj_three  35.4 us
    unnamed x29, local copies, waits for them, and re-layouts  30.3 us
    dot_general x3, matrix products, inverse(): jnp.einsum('...skm,srbm->...rkb', stacked, inner_inv, precision=HIGHEST)  30 us
  transfers between devices with their start and end apart: 22, of which 8 were waited for; matrix products, arithmetic and copies ran while one was open for 42% of the time, Pallas kernels for 0%

commit v1 on v0

--- a/solution.py
+++ b/solution.py
@@ -2,7 +2,10 @@
 
 import jax
 import jax.numpy as jnp
+import numpy as np
 from jax import lax
+from jax.experimental import pallas as pl
+from jax.experimental.pallas import tpu as pltpu
 from jax.sharding import PartitionSpec as P
 
 TIME_STEP = 0.1
@@ -123,7 +126,7 @@
     return grid.reshape(grid.shape[:-2] + (length,)) / length
 
 
-def shards(flux_perturbation, archived_nominal_heat_levels, archived_solidity_labels):
+def shards_general(flux_perturbation, archived_nominal_heat_levels, archived_solidity_labels):
     capacity = jnp.where(
         archived_solidity_labels == 0, 1.0, jnp.where(archived_solidity_labels == 1, 4.0, 1.25)
     ).astype(jnp.float32)
@@ -187,6 +190,261 @@
     return data_term + fourth_part + mixed_back
 
 
+OUTER = 16
+
+
+def half_spectrum(xs):
+    n = len(xs)
+    if n == 2:
+        return [(xs[0] + xs[1], None), (xs[0] - xs[1], None)]
+    even, odd = half_spectrum(xs[0::2]), half_spectrum(xs[1::2])
+    out = [None] * (n // 2 + 1)
+    for k in range(n // 4 + 1):
+        er, ei = even[k]
+        orr, oi = odd[k]
+        if k == 0:
+            out[0] = (er + orr, None)
+            out[n // 2] = (er - orr, None)
+        elif k == n // 4:
+            out[k] = (er, -orr)
+        else:
+            c, s = math.cos(2 * math.pi * k / n), math.sin(2 * math.pi * k / n)
+            if 8 * k == n:
+                tr, ti = c * (orr + oi), c * (oi - orr)
+            else:
+                tr, ti = c * orr + s * oi, c * oi - s * orr
+            out[k] = (er + tr, ei + ti)
+            out[n // 2 - k] = (er - tr, ti - ei)
+    return out
+
+
+def half_spectrum_t(gs):
+    half = len(gs) - 1
+    n = 2 * half
+    if n == 2:
+        return [gs[0][0] + gs[1][0], gs[0][0] - gs[1][0]]
+    even, odd = [], []
+    for m in range(n // 4 + 1):
+        gr, gi = gs[m]
+        if m == 0:
+            hr = gs[half][0]
+            even.append((gr + hr, None))
+            odd.append((gr - hr, None))
+        elif m == n // 4:
+            even.append((gr, None))
+            odd.append((-gi, None))
+        else:
+            hr, hi = gs[half - m]
+            even.append((gr + hr, gi - hi))
+            dr, di = gr - hr, gi + hi
+            c, s = math.cos(2 * math.pi * m / n), math.sin(2 * math.pi * m / n)
+            if 8 * m == n:
+                odd.append((c * (dr - di), c * (dr + di)))
+            else:
+                odd.append((c * dr - s * di, c * di + s * dr))
+    out = [None] * n
+    out[0::2] = half_spectrum_t(even)
+    out[1::2] = half_spectrum_t(odd)
+    return out
+
+
+def line_tables(length):
+    inner = length // OUTER
+    groups = OUTER // 2
+    b = np.arange(inner)[:, None]
+    mats = np.zeros((groups, 2 * inner, 2 * inner))
+    freq = np.zeros((groups, 2 * inner), np.int64)
+    scale = math.sqrt(2.0 / length)
+    for k1 in range(1, groups):
+        k = k1 + OUTER * np.arange(inner)
+        angle = 2.0 * math.pi * ((b * k[None, :]) % length) / length
+        c, s = np.cos(angle) * scale, np.sin(angle) * scale
+        mats[k1 - 1] = np.block([[c, -s], [s, c]])
+        freq[k1 - 1] = np.concatenate([k, k])
+    last = groups - 1
+    for part, first in ((0, 0), (1, groups)):
+        k = first + OUTER * np.arange(inner // 2)
+        angle = 2.0 * math.pi * ((b * k[None, :]) % length) / length
+        c, s = np.cos(angle) * scale, np.sin(angle) * scale
+        k_sin = k.copy()
+        if first == 0:
+            c[:, 0] = math.sqrt(1.0 / length)
+            k_sin[0] = length // 2
+            s[:, 0] = -math.sqrt(1.0 / length) * (1 - 2 * (np.arange(inner) % 2))
+        span = slice(part * inner, (part + 1) * inner)
+        mats[last][span, span] = np.concatenate([c, -s], axis=1)
+        freq[last][span] = np.concatenate([k, k_sin])
+    signed = np.where(freq < length // 2, freq, freq - length)
+    wave = (signed * (2.0 * math.pi / length)) ** 2
+    return mats, wave
+
+
+def two_parts(mats):
+    top = np.asarray(mats, np.float32).astype(jnp.bfloat16)
+    rest = (np.asarray(mats, np.float64) - top.astype(np.float64)).astype(jnp.bfloat16)
+    return top, rest
+
+
+def split(x):
+    top = x.astype(jnp.bfloat16)
+    return top, (x - top.astype(jnp.float32)).astype(jnp.bfloat16)
+
+
+def dot32(a, b):
+    return jnp.dot(a, b, preferred_element_type=jnp.float32)
+
+
+def right(x, hi, lo):
+    top, rest = split(x)
+    return dot32(top, hi) + (dot32(rest, hi) + dot32(top, lo))
+
+
+def left(hi, lo, x):
+    top, rest = split(x)
+    return dot32(hi, top) + (dot32(lo, top) + dot32(hi, rest))
+
+
+def pairs(spec):
+    ends = len(spec) - 1
+    return [spec[k] for k in range(1, ends)] + [(spec[0][0], spec[ends][0])]
+
+
+def unpairs(groups):
+    return [(groups[-1][0], None)] + groups[:-1] + [(groups[-1][1], None)]
+
+
+def y_forward(x_ref, hi_ref, lo_ref, out_ref):
+    parts, wide = x_ref.shape[0], x_ref.shape[-1]
+    inner = parts * wide // OUTER
+    per = wide // inner
+    xs = [x_ref[a // per, 0, :, (a % per) * inner : (a % per + 1) * inner] for a in range(OUTER)]
+    width = out_ref.shape[-1]
+    each = 2 * inner // width
+    for g, (re, im) in enumerate(pairs(half_spectrum(xs))):
+        res = right(jnp.concatenate([re, im], axis=1), hi_ref[g], lo_ref[g])
+        for c in range(each):
+            out_ref[g * each + c, 0] = res[:, c * width : (c + 1) * width]
+
+
+def y_inverse(x_ref, hi_ref, lo_ref, out_ref):
+    parts, wide = out_ref.shape[0], out_ref.shape[-1]
+    inner = parts * wide // OUTER
+    per = wide // inner
+    width = x_ref.shape[-1]
+    each = 2 * inner // width
+    groups = []
+    for g in range(OUTER // 2):
+        spec = jnp.concatenate([x_ref[g * each + c, 0] for c in range(each)], axis=1)
+        res = right(spec, hi_ref[g], lo_ref[g])
+        groups.append((res[:, :inner], res[:, inner:]))
+    for a, slab in enumerate(half_spectrum_t(unpairs(groups))):
+        out_ref[a // per, 0, :, (a % per) * inner : (a % per + 1) * inner] = slab
+
+
+def x_apply(x_ref, ky_ref, kx_ref, fhi_ref, flo_ref, ihi_ref, ilo_ref, out_ref):
+    count, nvec, rows, width = x_ref.shape
+    inner = count * rows // OUTER
+    per = inner // rows
+
+    def slab(a):
+        return jnp.concatenate(
+            [x_ref[a * per : (a + 1) * per, v].reshape(inner, width) for v in range(nvec)], axis=1
+        )
+
+    ky = jnp.concatenate([ky_ref[...]] * nvec, axis=1)
+    groups = []
+    for g, (re, im) in enumerate(pairs(half_spectrum([slab(a) for a in range(OUTER)]))):
+        spec = left(fhi_ref[g], flo_ref[g], jnp.concatenate([re, im], axis=0))
+        wave = kx_ref[g] + ky
+        res = left(ihi_ref[g], ilo_ref[g], PRIOR_GAIN * wave * wave * spec)
+        groups.append((res[:inner], res[inner:]))
+    for a, res in enumerate(half_spectrum_t(unpairs(groups))):
+        for v in range(nvec):
+            out_ref[a * per : (a + 1) * per, v] = res[:, v * width : (v + 1) * width].reshape(
+                per, rows, width
+            )
+
+
+def prior(q):
+    across, along = lax.axis_size("gx"), lax.axis_size("gy")
+    nvec, bx, by = q.shape
+    length = by * along
+    count = across * along
+    rows = bx // along
+    width = length // count
+    mats, wave = line_tables(length)
+    fhi, flo = two_parts(mats)
+    thi, tlo = two_parts(np.swapaxes(mats, 1, 2))
+    params = pltpu.CompilerParams(vmem_limit_bytes=58 * 2**20)
+    table = pl.BlockSpec(fhi.shape, lambda v: (0, 0, 0))
+    lines = pl.BlockSpec((along, 1, rows, by), lambda v: (0, v, 0, 0))
+    packed = pl.BlockSpec((count, 1, rows, width), lambda v: (0, v, 0, 0))
+    lines_shape = jax.ShapeDtypeStruct((along, nvec, rows, by), jnp.float32)
+    packed_shape = jax.ShapeDtypeStruct((count, nvec, rows, width), jnp.float32)
+
+    send = jnp.swapaxes(q.reshape(nvec, along, rows, by), 0, 1)
+    whole_y = lax.all_to_all(send, "gy", 0, 0, tiled=True)
+    spec_y = pl.pallas_call(
+        y_forward, grid=(nvec,), in_specs=[lines, table, table], out_specs=packed,
+        out_shape=packed_shape, compiler_params=params, name="y_forward",
+    )(whole_y, fhi, flo)
+    whole_x = lax.all_to_all(spec_y, ("gx", "gy"), 0, 0, tiled=True)
+    me = lax.axis_index("gx") * along + lax.axis_index("gy")
+    ky = lax.dynamic_slice_in_dim(
+        jnp.asarray(wave.reshape(1, length), jnp.float32), me * width, width, axis=1
+    )
+    kx = jnp.asarray(wave[:, :, None], jnp.float32)
+    done_x = pl.pallas_call(
+        x_apply, out_shape=packed_shape, compiler_params=params, name="x_apply",
+    )(whole_x, ky, kx, thi, tlo, fhi, flo)
+    back_y = lax.all_to_all(done_x, ("gx", "gy"), 0, 0, tiled=True)
+    done_y = pl.pallas_call(
+        y_inverse, grid=(nvec,), in_specs=[packed, table, table], out_specs=lines,
+        out_shape=lines_shape, compiler_params=params, name="y_inverse",
+    )(back_y, thi, tlo)
+    back = lax.all_to_all(done_y, "gy", 0, 0, tiled=True)
+    return jnp.swapaxes(back, 0, 1).reshape(nvec, bx, by)
+
+
+def data_term(flux_perturbation, archived_nominal_heat_levels, archived_solidity_labels):
+    capacity = jnp.where(
+        archived_solidity_labels == 0, 1.0, jnp.where(archived_solidity_labels == 1, 4.0, 1.25)
+    ).astype(jnp.float32)
+    diffusion_advance = jnp.where(
+        archived_solidity_labels == 0, 1.0, jnp.where(archived_solidity_labels == 1, 0.6, 0.35)
+    ).astype(jnp.float32)
+    diffusion_advance = diffusion_advance * (1.0 + 0.5 * jnp.tanh(archived_nominal_heat_levels))
+    first_u = TIME_STEP * flux_perturbation / capacity[0, 0]
+    second_top = TIME_STEP * flux_perturbation + TIME_STEP * (
+        diffusion_advance[0, 0] * (surface_rim(first_u) - 6.0 * first_u) + flux_perturbation
+    )
+    second_low = TIME_STEP * diffusion_advance[0, 1] * first_u
+    top_u = second_top / capacity[1, 0]
+    low_u = second_low / capacity[1, 1]
+    third_top = second_top + TIME_STEP * (
+        diffusion_advance[1, 0] * (surface_rim(top_u) - 6.0 * top_u + low_u) + flux_perturbation
+    )
+    misfit = OBS_WEIGHT * third_top / capacity[1, 0]
+    adj_three = misfit / capacity[1, 0]
+    push_top = TIME_STEP * diffusion_advance[1, 0] * adj_three
+    adj_two_top = adj_three + (surface_rim(push_top) - 6.0 * push_top) / capacity[1, 0]
+    adj_two_low = push_top / capacity[1, 1]
+    pull_top = TIME_STEP * diffusion_advance[0, 0] * adj_two_top
+    pull_low = TIME_STEP * diffusion_advance[0, 1] * adj_two_low
+    adj_one_top = adj_two_top + (surface_rim(pull_top) - 6.0 * pull_top + pull_low) / capacity[0, 0]
+    return TIME_STEP * (adj_three + adj_two_top + adj_one_top)
+
+
+def shards(q, heat, labels):
+    nvec, bx, by = q.shape
+    along, across = lax.axis_size("gy"), lax.axis_size("gx")
+    rows, width = bx // along, by // across
+    square = bx * across == by * along
+    if not square or rows % 16 or width % 128 or by % (by * along // OUTER):
+        return shards_general(q, heat, labels)
+    return data_term(q, heat, labels) + prior(q)
+
+
 def solution(mesh):
     in_specs = (P(None, "gx", "gy"), P(None, None, "gx", "gy"), P(None, None, "gx", "gy"))
     out_specs = P(None, "gx", "gy")

time: 823 us -> 442 us (0.54)
  local copies, waits for them, and re-layouts: 244 us -> 22.4 us
  matrix products: 125 us -> 0 us
  other arithmetic: 150 us -> 94.2 us
  blocking collectives: 0 us -> 51.2 us
  waiting for transfers between devices: 208 us -> 166 us
  Pallas kernels: 0 us -> 37.5 us
  starting transfers between devices: 88.5 us -> 67.4 us
    dot_general x12 -> x0, matrix products: 125 us -> none  [the longest x3 41.5 us: forward(): jnp.einsum('...rkb,rsbm->...skm', twisted, inner_fwd, precision=HIGHEST)]
    all_to_all x6 -> x3, waiting for transfers between devices: 187 us -> 89.6 us  [the longest x1 89.6 us: prior(): whole_x = lax.all_to_all(spec_y, ('gx', 'gy'), 0, 0, tiled=True)]
    all_to_all x14 -> x0, local copies, waits for them, and re-layouts: 74.8 us -> none  [the longest x3 17.3 us: shards(): lax.all_to_all(second_x, 'gx', split_axis=1, concat_axis=2, tiled=True)]
    ppermute x8, waiting for transfers between devices: 5.11 us -> 68.6 us  [with_halo(): lax.ppermute(tail, axis, [(i, (i + 1) % count) for i in range(ends)])]
    all_to_all x0 -> x1, blocking collectives: none -> 51.2 us  [prior(): whole_y = lax.all_to_all(send, 'gy', 0, 0, tiled=True)]
    pallas_call x0 -> x3, Pallas kernels: none -> 37.5 us  [the longest x1 18.4 us: prior(): pl.pallas_call(x_apply, out_shape=packed_shape, compiler_params=params, n...]
    div x8 -> x1, local copies, waits for them, and re-layouts: 34.1 us -> 2.59 us  [data_term(): top_u = second_top / capacity[1, 0]]
    transpose x2 -> x1, local copies, waits for them, and re-layouts: 32.5 us -> 4.86 us  [prior(): return jnp.swapaxes(back, 0, 1).reshape(nvec, bx, by)]
  transfers between devices with their start and end apart: 22 -> 19, of which waited for: 8 -> 6; matrix products, arithmetic and copies ran while one was open for 42% -> 21% of each run, Pallas kernels for 0% -> 0%
where the time goes in v1:
time: 442 us; the launch traced here: 439 us
  waiting for transfers between devices  166 us (38%)
  other arithmetic  94.2 us (21%)
  starting transfers between devices  67.4 us (15%)
  blocking collectives  51.2 us (12%)
  Pallas kernels  37.5 us (8%)
  local copies, waits for them, and re-layouts  22.4 us (5%)
    all_to_all x1, waiting for transfers between devices, prior(): whole_x = lax.all_to_all(spec_y, ('gx', 'gy'), 0, 0, tiled=True)  89.6 us
    ppermute x8, waiting for transfers between devices, with_halo(): lax.ppermute(tail, axis, [(i, (i + 1) % count) for i in range(ends)])  68.6 us
    all_to_all x1, blocking collectives, prior(): whole_y = lax.all_to_all(send, 'gy', 0, 0, tiled=True)  51.2 us
    mul x2, other arithmetic, data_term(): push_top = TIME_STEP * diffusion_advance[1, 0] * adj_three  31 us
    ppermute x8, starting transfers between devices, with_halo(): lax.ppermute(tail, axis, [(i, (i + 1) % count) for i in range(ends)])  26.1 us
    ppermute x8, starting transfers between devices, with_halo(): lax.ppermute(head, axis, [((i + 1) % count, i) for i in range(ends)])  23.6 us
    pallas_call x1, Pallas kernels, prior(): pl.pallas_call(x_apply, out_shape=packed_shape, compiler_params=params, n...  18.4 us
    mul x1, other arithmetic, data_term(): pull_top = TIME_STEP * diffusion_advance[0, 0] * adj_two_top  13.8 us
  transfers between devices with their start and end apart: 19, of which 6 were waited for; matrix products, arithmetic and copies ran while one was open for 21% of the time, Pallas kernels for 0%

profile of v1, /device:TPU:17, one launch (start us, length us, event | category | flops | bytes accessed | tf_op | source)
XLA Modules:
  0.0 439.1 jit_solution(3450299593117763704)
XLA Ops:
  0.0 2.5 copy.31
  2.5 51.2 %all_to_all.20.x_ref = f32[4,2,128,1024]{3,2,1,0:T(8,128)} all-to-all(f32[4,2,128,1024]{3,2,1,0:T(8,128)S(1)} %bitcast.26), channel_id=1, replica_groups=mesh['gx'=8,'gy'=4] {'gy'}, dimensions={0} | all-to-all | bytes 8388608 | tf_op jit(solution)/shard_map/all_to_all | solution.py:386
  53.7 9.5 %y_forward.1 = f32[32,2,128,128]{3,2,1,0:T(8,128)} custom-call(f32[4,2,128,1024]{3,2,1,0:T(8,128)} %all_to_all.20.x_ref, bf16[8,512,512]{2,1,0:T(8,128)(2,1)} %constant.52.clone.hi_ref.ihi_ref, bf16[8,512,512]{2,1,0:T(8,128)(2,1)} %constant.53.clone.lo_ref.ilo_ref), custom_call_target="tpu_custom_call" | custom-call | tf_op jit(solution)/shard_map/y_forward/pallas_call | solution.py:387
  63.3 5.8 %all-to-all-start.1 = ((f32[32,2,128,128]{3,2,1,0:T(8,128)}), f32[32,2,128,128]{3,2,1,0:T(8,128)}, u32[]{:S(2)}, u32[]{:S(2)}) async-start(f32[32,2,128,128]{3,2,1,0:T(8,128)} %y_forward.1), calls=%async_computation.1 | async-start | bytes 8388608 | tf_op jit(solution)/shard_map/all_to_all | solution.py:391
  69.0 1.3 constant_dynamic-slice_fusion.ky_ref
  70.3 89.6 %all-to-all-done.1.x_ref = f32[32,2,128,128]{3,2,1,0:T(8,128)} async-done(((f32[32,2,128,128]{3,2,1,0:T(8,128)}), f32[32,2,128,128]{3,2,1,0:T(8,128)}, u32[]{:S(2)}, u32[]{:S(2)}) %all-to-all-start.1) | async-done | bytes 4194336 | tf_op jit(solution)/shard_map/all_to_all | solution.py:391
  159.9 18.4 %x_apply.1 = f32[32,2,128,128]{3,2,1,0:T(8,128)} custom-call(f32[32,2,128,128]{3,2,1,0:T(8,128)} %all-to-all-done.1.x_ref, f32[1,128]{1,0:T(1,128)} %constant_dynamic-slice_fusion.ky_ref, f32[8,512,1]{2,1,0:T(8,128)} %constant.55.clone.kx_ref, bf16[8,512,512]{2,1,0:T(8,128)(2,1)} %constant.56.clone.fhi_ref.hi_ref, ...), custom_call_target="tpu_custom_call" | custom-call | tf_op jit(solution)/shard_map/x_apply/pallas_call | solution.py:397
  178.3 7.1 %all-to-all-start.2 = ((f32[32,2,128,128]{3,2,1,0:T(8,128)}), f32[32,2,128,128]{3,2,1,0:T(8,128)}, u32[]{:S(2)}, u32[]{:S(2)}) async-start(f32[32,2,128,128]{3,2,1,0:T(8,128)} %x_apply.1), calls=%async_computation.2 | async-start | bytes 8388608 | tf_op jit(solution)/shard_map/all_to_all | solution.py:400
  185.4 9.8 %add_multiply_fusion = (f32[2,2,512,1024]{3,2,1,0:T(8,128)}, pred[2,2,512,1024]{3,2,1,0:T(8,128)(4,1)S(1)}, pred[2,2,512,1024]{3,2,1,0:T(8,128)(4,1)S(1)}) fusion(f32[2,2,512,1024]{3,2,1,0:T(8,128)} %param.10, s32[2,2,512,1024]{3,2,1,0:T(8,128)} %param.11), kind=kLoop, calls=%fused_computation.1 | loop fusion | flops 14680064 | bytes 29360128 | tf_op jit(solution)/shard_map/mul | solution.py:416
  195.1 1.6 select_select_fusion
  196.8 2.6 slice_bitcast_fusion.1
  199.4 3.0 copy-done.7
  202.3 1.0 multiply_divide_fusion
  203.3 3.1 collective-permute-start.1
  206.5 3.1 collective-permute-start
  209.5 68.3 %collective-permute-done.1 = f32[2,1,1024]{2,1,0:T(1,128)S(1)} collective-permute-done((f32[2,1,1024]{2,1,0:T(1,128)S(1)}, f32[2,1,1024]{2,1,0:T(1,128)S(1)}, u32[]{:S(2)}, u32[]{:S(2)}) %collective-permute-start.1) | collective-permute-done | bytes 8224 | tf_op jit(solution)/shard_map/ppermute | solution.py:25
  277.9 0.2 pad_maximum_fusion.43
  278.1 0.2 copy.12
  278.3 0.2 copy.14
  278.6 4.0 collective-permute-start.3
  282.5 1.9 collective-permute-start.2
  284.5 5.8 %slice_bitcast_fusion.2 = (f32[512,1024]{1,0:T(8,128)}, f32[512,1024]{1,0:T(8,128)}, f32[512,1024]{1,0:T(8,128)}) fusion(f32[2,2,512,1024]{3,2,1,0:T(8,128)} %get-tuple-element.9), kind=kLoop, calls=%fused_computation.76 | loop fusion | flops 524288 | bytes 12582912 | tf_op jit(solution)/shard_map/mul | solution.py:425
  290.3 0.2 copy.13
  290.6 0.2 copy.15
  290.8 13.4 %broadcast_divide_fusion = f32[2,512,1024]{2,1,0:T(8,128)S(1)} fusion(f32[512,1024]{1,0:T(8,128)} %get-tuple-element.15, f32[2,512,1024]{2,1,0:T(8,128)} %param.9, f32[2,512,1024]{2,1,0:T(8,128)} %copy-done, f32[2,1,1024]{2,1,0:T(1,128)S(1)} %collective-permute-done, f32[2,1,1024]{2,1,0:T(1,128)S(1)} %collective-permute-done.1, f32[2,514,1]{2,1,0:T(8,128)S(1)} %copy.15, ...), kind=kLoop, calls=%fused_computation.81 | loop fusion | flops 19922944 | bytes 16801824 | tf_op jit(solution)/shard_map/div | solution.py:422
  304.2 1.9 collective-permute-start.5
  306.1 4.3 collective-permute-start.4
  310.4 5.1 %broadcast_multiply_fusion.3 = (f32[512,1024]{1,0:T(8,128)}, f32[512,1024]{1,0:T(8,128)}) fusion(f32[2,2,512,1024]{3,2,1,0:T(8,128)} %get-tuple-element.9), kind=kLoop, calls=%fused_computation.83 | loop fusion | flops 1048576 | bytes 8388608 | tf_op jit(solution)/shard_map/mul | solution.py:429
  315.6 1.2 pad_maximum_fusion.40
  316.7 1.3 copy.16
  318.0 1.3 copy.18
  319.3 4.2 collective-permute-start.7
  323.5 2.1 collective-permute-start.6
  325.6 3.2 fusion.34
  328.8 1.0 copy.17
  329.9 1.0 copy.19
  330.9 9.6 %y_inverse.1 = f32[4,2,128,1024]{3,2,1,0:T(8,128)} custom-call(f32[32,2,128,128]{3,2,1,0:T(8,128)} %all-to-all-done.2.x_ref, bf16[8,512,512]{2,1,0:T(8,128)(2,1)} %constant.56.clone.fhi_ref.hi_ref, bf16[8,512,512]{2,1,0:T(8,128)(2,1)} %constant.57.clone.flo_ref.lo_ref), custom_call_target="tpu_custom_call" | custom-call | tf_op jit(solution)/shard_map/y_inverse/pallas_call | solution.py:401
  340.5 4.9 %all-to-all-start.3 = ((f32[4,2,128,1024]{3,2,1,0:T(8,128)}), f32[4,2,128,1024]{3,2,1,0:T(8,128)}, u32[]{:S(2)}, u32[]{:S(2)}) async-start(f32[4,2,128,1024]{3,2,1,0:T(8,128)} %y_inverse.1), calls=%async_computation.3 | async-start | bytes 8388608 | tf_op jit(solution)/shard_map/all_to_all | solution.py:405
  345.4 25.8 %broadcast_multiply_fusion.1 = (f32[2,512,1024]{2,1,0:T(8,128)S(1)}, f32[2,512,1024]{2,1,0:T(8,128)}) fusion(f32[512,1024]{1,0:T(8,128)} %get-tuple-element.18, f32[512,1024]{1,0:T(8,128)} %fusion.34, f32[2,512,1024]{2,1,0:T(8,128)} %param.9, f32[512,1024]{1,0:T(8,128)} %get-tuple-element.16, f32[512,1024]{1,0:T(8,128)S(1)} %get-tuple-element.17, ...), kind=kLoop, calls=%fused_computation.80 | loop fusion | flops 44040192 | bytes 35700800 | tf_op jit(solution)/shard_map/mul | solution.py:429
  371.3 2.3 collective-permute-start.9
  373.6 4.1 collective-permute-start.8
  377.7 0.8 collective-permute-done.8
  378.5 0.2 pad_maximum_fusion.37
  378.7 0.2 copy.20
  379.0 1.9 collective-permute-start.10
  380.9 0.2 copy.22
  381.1 4.8 %collective-permute-start.11 = (f32[2,514,1]{1,0,2:T(2,128)S(1)}, f32[2,514,1]{1,0,2:T(2,128)S(1)}, u32[]{:S(2)}, u32[]{:S(2)}) collective-permute-start(f32[2,514,1]{1,0,2:T(2,128)S(1)} %copy.22), channel_id=1, source_target_pairs={{0,1},{1,2},{2,3},{4,5},{5,6},{6,7},{8,9},{9,10},{10,11},{12,13},{... | collective-permute-start | bytes 12344 | tf_op jit(solution)/shard_map/ppermute | solution.py:25
  385.9 6.2 %collective-permute-done.10 = f32[2,514,1]{1,0,2:T(2,128)S(1)} collective-permute-done((f32[2,514,1]{1,0,2:T(2,128)S(1)}, f32[2,514,1]{1,0,2:T(2,128)S(1)}, u32[]{:S(2)}, u32[]{:S(2)}) %collective-permute-start.10) | collective-permute-done | bytes 4144 | tf_op jit(solution)/shard_map/ppermute | solution.py:27
  392.0 0.2 copy.21
  392.3 0.2 copy.23
  392.5 13.8 %broadcast_multiply_fusion = (f32[2,512,1024]{2,1,0:T(8,128)S(1)}, f32[2,512,1024]{2,1,0:T(8,128)}) fusion(f32[512,1024]{1,0:T(8,128)} %get-tuple-element.19, f32[2,512,1024]{2,1,0:T(8,128)} %get-tuple-element.8, f32[512,1024]{1,0:T(8,128)S(1)} %copy-done.8, f32[2,512,1024]{2,1,0:T(8,128)} %copy-done.3, f32[2,1,1024]{2,1,0:T(1,128)S(1)} %collective-permute-done.8, ...), kind=kLoop, calls=%fused_computation.79 | loop fusion | flops 16777216 | bytes 20996128 | tf_op jit(solution)/shard_map/mul | solution.py:432
  406.4 1.9 collective-permute-start.13
  408.3 4.3 collective-permute-start.12
  412.6 0.8 collective-permute-done.12
  413.3 0.2 pad_maximum_fusion.34
  413.6 0.2 copy.24
  413.8 1.9 collective-permute-start.14
  415.7 0.2 copy.26
  416.0 3.9 collective-permute-start.15
  419.9 0.2 copy.25
  420.1 0.2 collective-permute-done.15
  420.3 1.0 copy.27
  421.4 4.9 %copy.29 = f32[2,4,128,1024]{3,2,1,0:T(8,128)} copy(f32[2,4,128,1024]{3,2,0,1:T(8,128)} %bitcast.8) | data formatting | bytes 8388608 | tf_op jit(solution)/shard_map/transpose | solution.py:406
  426.2 12.8 %bitcast_add_fusion = f32[2,512,1024]{2,1,0:T(8,128)} fusion(f32[2,4,128,1024]{3,2,1,0:T(8,128)} %copy.29, f32[2,512,1024]{2,1,0:T(8,128)} %get-tuple-element.6, f32[2,512,1024]{2,1,0:T(8,128)S(1)} %copy-done.5, f32[2,1,1024]{2,1,0:T(1,128)S(1)} %collective-permute-done.12, f32[2,1,1024]{2,1,0:T(1,128)S(1)} %collective-permute-done.13, ...), kind=kLoop, calls=%fused_computation.67 | loop fusion | flops 24117248 | bytes 29384736 | tf_op jit(solution)/shard_map/add | solution.py:445
  (34 shorter events, 0.1 us)
Async XLA Ops:
  63.3 96.6 %all-to-all-start.1 = ((f32[32,2,128,128]{3,2,1,0:T(8,128)}), f32[32,2,128,128]{3,2,1,0:T(8,128)}, u32[]{:S(2)}, u32[]{:S(2)}) async-start(f32[32,2,128,128]{3,2,1,0:T(8,128)} %y_forward.1), calls=%async_computation.1 | async-start | bytes 8388608 | tf_op jit(solution)/shard_map/all_to_all | solution.py:391
  178.3 152.7 %all-to-all-start.2 = ((f32[32,2,128,128]{3,2,1,0:T(8,128)}), f32[32,2,128,128]{3,2,1,0:T(8,128)}, u32[]{:S(2)}, u32[]{:S(2)}) async-start(f32[32,2,128,128]{3,2,1,0:T(8,128)} %x_apply.1), calls=%async_computation.2 | async-start | bytes 8388608 | tf_op jit(solution)/shard_map/all_to_all | solution.py:400
  196.8 5.6 %copy-start.7 = (f32[2,2,512,1024]{3,2,1,0:T(8,128)}, f32[2,2,512,1024]{3,2,1,0:T(8,128)S(1)}, u32[]{:S(2)}) copy-start(f32[2,2,512,1024]{3,2,1,0:T(8,128)S(1)} %select_select_fusion) | copy-start | bytes 25165828
  196.8 5.6 %copy-start.1 = (f32[2,512,1024]{2,1,0:T(8,128)S(1)}, f32[2,512,1024]{2,1,0:T(8,128)}, u32[]{:S(2)}) copy-start(f32[2,512,1024]{2,1,0:T(8,128)} %param.9) | copy-start | bytes 12582916
  202.3 143.1 %copy-start.6 = (f32[512,1024]{1,0:T(8,128)}, f32[512,1024]{1,0:T(8,128)S(1)}, u32[]{:S(2)}) copy-start(f32[512,1024]{1,0:T(8,128)S(1)} %get-tuple-element.17) | copy-start | bytes 6291460
  203.3 74.6 %copy-start = (f32[2,512,1024]{2,1,0:T(8,128)}, f32[2,512,1024]{2,1,0:T(8,128)S(1)}, u32[]{:S(2)}) copy-start(f32[2,512,1024]{2,1,0:T(8,128)S(1)} %multiply_divide_fusion) | copy-start | bytes 12582916
  203.3 74.5 %collective-permute-start.1 = (f32[2,1,1024]{2,1,0:T(1,128)S(1)}, f32[2,1,1024]{2,1,0:T(1,128)S(1)}, u32[]{:S(2)}, u32[]{:S(2)}) collective-permute-start(f32[2,1,1024]{2,1,0:T(1,128)S(1)} %get-tuple-element.34), channel_id=1, source_target_pairs={{0,4},{4,8},{8,12},{12,16},{16,20},{20,24},{24,28},{1,5},{5,9},{9,... | collective-permute-start | bytes 24584 | tf_op jit(solution)/shard_map/ppermute | solution.py:25
  206.5 71.4 %collective-permute-start = (f32[2,1,1024]{2,1,0:T(1,128)S(1)}, f32[2,1,1024]{2,1,0:T(1,128)S(1)}, u32[]{:S(2)}, u32[]{:S(2)}) collective-permute-start(f32[2,1,1024]{2,1,0:T(1,128)S(1)} %get-tuple-element.35), channel_id=1, source_target_pairs={{4,0},{8,4},{12,8},{16,12},{20,16},{24,20},{28,24},{5,1},{9,5},{13... | collective-permute-start | bytes 24584 | tf_op jit(solution)/shard_map/ppermute | solution.py:27
  278.6 12.0 %collective-permute-start.3 = (f32[2,514,1]{1,0,2:T(2,128)S(1)}, f32[2,514,1]{1,0,2:T(2,128)S(1)}, u32[]{:S(2)}, u32[]{:S(2)}) collective-permute-start(f32[2,514,1]{1,0,2:T(2,128)S(1)} %copy.14), channel_id=1, source_target_pairs={{0,1},{1,2},{2,3},{4,5},{5,6},{6,7},{8,9},{9,10},{10,11},{12,13},{... | collective-permute-start | bytes 12344 | tf_op jit(solution)/shard_map/ppermute | solution.py:25
  282.5 7.8 %collective-permute-start.2 = (f32[2,514,1]{1,0,2:T(2,128)S(1)}, f32[2,514,1]{1,0,2:T(2,128)S(1)}, u32[]{:S(2)}, u32[]{:S(2)}) collective-permute-start(f32[2,514,1]{1,0,2:T(2,128)S(1)} %copy.12), channel_id=1, source_target_pairs={{1,0},{2,1},{3,2},{5,4},{6,5},{7,6},{9,8},{10,9},{11,10},{13,12},{... | collective-permute-start | bytes 12344 | tf_op jit(solution)/shard_map/ppermute | solution.py:27
  304.2 11.4 %copy-start.2 = (f32[2,512,1024]{2,1,0:T(8,128)}, f32[2,512,1024]{2,1,0:T(8,128)S(1)}, u32[]{:S(2)}) copy-start(f32[2,512,1024]{2,1,0:T(8,128)S(1)} %broadcast_divide_fusion) | copy-start | bytes 12582916
  304.2 11.3 %collective-permute-start.5 = (f32[2,1,1024]{2,1,0:T(1,128)S(1)}, f32[2,1,1024]{2,1,0:T(1,128)S(1)}, u32[]{:S(2)}, u32[]{:S(2)}) collective-permute-start(f32[2,1,1024]{2,1,0:T(1,128)S(1)} %get-tuple-element.32), channel_id=1, source_target_pairs={{0,4},{4,8},{8,12},{12,16},{16,20},{20,24},{24,28},{1,5},{5,9},{9,... | collective-permute-start | bytes 24584 | tf_op jit(solution)/shard_map/ppermute | solution.py:25
  306.1 9.4 %collective-permute-start.4 = (f32[2,1,1024]{2,1,0:T(1,128)S(1)}, f32[2,1,1024]{2,1,0:T(1,128)S(1)}, u32[]{:S(2)}, u32[]{:S(2)}) collective-permute-start(f32[2,1,1024]{2,1,0:T(1,128)S(1)} %get-tuple-element.33), channel_id=1, source_target_pairs={{4,0},{8,4},{12,8},{16,12},{20,16},{24,20},{28,24},{5,1},{9,5},{13... | collective-permute-start | bytes 24584 | tf_op jit(solution)/shard_map/ppermute | solution.py:27
  319.3 10.6 %collective-permute-start.7 = (f32[2,514,1]{1,0,2:T(2,128)S(1)}, f32[2,514,1]{1,0,2:T(2,128)S(1)}, u32[]{:S(2)}, u32[]{:S(2)}) collective-permute-start(f32[2,514,1]{1,0,2:T(2,128)S(1)} %copy.18), channel_id=1, source_target_pairs={{0,1},{1,2},{2,3},{4,5},{5,6},{6,7},{8,9},{9,10},{10,11},{12,13},{... | collective-permute-start | bytes 12344 | tf_op jit(solution)/shard_map/ppermute | solution.py:25
  323.5 5.4 %collective-permute-start.6 = (f32[2,514,1]{1,0,2:T(2,128)S(1)}, f32[2,514,1]{1,0,2:T(2,128)S(1)}, u32[]{:S(2)}, u32[]{:S(2)}) collective-permute-start(f32[2,514,1]{1,0,2:T(2,128)S(1)} %copy.16), channel_id=1, source_target_pairs={{1,0},{2,1},{3,2},{5,4},{6,5},{7,6},{9,8},{10,9},{11,10},{13,12},{... | collective-permute-start | bytes 12344 | tf_op jit(solution)/shard_map/ppermute | solution.py:27
  340.5 80.9 %all-to-all-start.3 = ((f32[4,2,128,1024]{3,2,1,0:T(8,128)}), f32[4,2,128,1024]{3,2,1,0:T(8,128)}, u32[]{:S(2)}, u32[]{:S(2)}) async-start(f32[4,2,128,1024]{3,2,1,0:T(8,128)} %y_inverse.1), calls=%async_computation.3 | async-start | bytes 8388608 | tf_op jit(solution)/shard_map/all_to_all | solution.py:405
  371.2 7.3 %copy-start.3 = (f32[2,512,1024]{2,1,0:T(8,128)}, f32[2,512,1024]{2,1,0:T(8,128)S(1)}, u32[]{:S(2)}) copy-start(f32[2,512,1024]{2,1,0:T(8,128)S(1)} %get-tuple-element.7) | copy-start | bytes 12582916
  371.2 21.3 %copy-start.8 = (f32[512,1024]{1,0:T(8,128)S(1)}, f32[512,1024]{1,0:T(8,128)}, u32[]{:S(2)}) copy-start(f32[512,1024]{1,0:T(8,128)} %get-tuple-element.15) | copy-start | bytes 6291460
  371.3 6.5 %collective-permute-start.9 = (f32[2,1,1024]{2,1,0:T(1,128)S(1)}, f32[2,1,1024]{2,1,0:T(1,128)S(1)}, u32[]{:S(2)}, u32[]{:S(2)}) collective-permute-start(f32[2,1,1024]{2,1,0:T(1,128)S(1)} %get-tuple-element.30), channel_id=1, source_target_pairs={{0,4},{4,8},{8,12},{12,16},{16,20},{20,24},{24,28},{1,5},{5,9},{9,... | collective-permute-start | bytes 24584 | tf_op jit(solution)/shard_map/ppermute | solution.py:25
  373.6 4.9 %collective-permute-start.8 = (f32[2,1,1024]{2,1,0:T(1,128)S(1)}, f32[2,1,1024]{2,1,0:T(1,128)S(1)}, u32[]{:S(2)}, u32[]{:S(2)}) collective-permute-start(f32[2,1,1024]{2,1,0:T(1,128)S(1)} %get-tuple-element.31), channel_id=1, source_target_pairs={{4,0},{8,4},{12,8},{16,12},{20,16},{24,20},{28,24},{5,1},{9,5},{13... | collective-permute-start | bytes 24584 | tf_op jit(solution)/shard_map/ppermute | solution.py:27
  379.0 13.1 %collective-permute-start.10 = (f32[2,514,1]{1,0,2:T(2,128)S(1)}, f32[2,514,1]{1,0,2:T(2,128)S(1)}, u32[]{:S(2)}, u32[]{:S(2)}) collective-permute-start(f32[2,514,1]{1,0,2:T(2,128)S(1)} %copy.20), channel_id=1, source_target_pairs={{1,0},{2,1},{3,2},{5,4},{6,5},{7,6},{9,8},{10,9},{11,10},{13,12},{... | collective-permute-start | bytes 12344 | tf_op jit(solution)/shard_map/ppermute | solution.py:27
  381.1 11.2 %collective-permute-start.11 = (f32[2,514,1]{1,0,2:T(2,128)S(1)}, f32[2,514,1]{1,0,2:T(2,128)S(1)}, u32[]{:S(2)}, u32[]{:S(2)}) collective-permute-start(f32[2,514,1]{1,0,2:T(2,128)S(1)} %copy.22), channel_id=1, source_target_pairs={{0,1},{1,2},{2,3},{4,5},{5,6},{6,7},{8,9},{9,10},{10,11},{12,13},{... | collective-permute-start | bytes 12344 | tf_op jit(solution)/shard_map/ppermute | solution.py:25
  406.4 7.0 %copy-start.4 = (f32[2,512,1024]{2,1,0:T(8,128)}, f32[2,512,1024]{2,1,0:T(8,128)S(1)}, u32[]{:S(2)}) copy-start(f32[2,512,1024]{2,1,0:T(8,128)S(1)} %get-tuple-element.5) | copy-start | bytes 12582916
  406.4 6.2 %collective-permute-start.13 = (f32[2,1,1024]{2,1,0:T(1,128)S(1)}, f32[2,1,1024]{2,1,0:T(1,128)S(1)}, u32[]{:S(2)}, u32[]{:S(2)}) collective-permute-start(f32[2,1,1024]{2,1,0:T(1,128)S(1)} %get-tuple-element.28), channel_id=1, source_target_pairs={{0,4},{4,8},{8,12},{12,16},{16,20},{20,24},{24,28},{1,5},{5,9},{9,... | collective-permute-start | bytes 24584 | tf_op jit(solution)/shard_map/ppermute | solution.py:25
  408.3 5.0 %collective-permute-start.12 = (f32[2,1,1024]{2,1,0:T(1,128)S(1)}, f32[2,1,1024]{2,1,0:T(1,128)S(1)}, u32[]{:S(2)}, u32[]{:S(2)}) collective-permute-start(f32[2,1,1024]{2,1,0:T(1,128)S(1)} %get-tuple-element.29), channel_id=1, source_target_pairs={{4,0},{8,4},{12,8},{16,12},{20,16},{24,20},{28,24},{5,1},{9,5},{13... | collective-permute-start | bytes 24584 | tf_op jit(solution)/shard_map/ppermute | solution.py:27
  413.8 6.1 %collective-permute-start.14 = (f32[2,514,1]{1,0,2:T(2,128)S(1)}, f32[2,514,1]{1,0,2:T(2,128)S(1)}, u32[]{:S(2)}, u32[]{:S(2)}) collective-permute-start(f32[2,514,1]{1,0,2:T(2,128)S(1)} %copy.24), channel_id=1, source_target_pairs={{1,0},{2,1},{3,2},{5,4},{6,5},{7,6},{9,8},{10,9},{11,10},{13,12},{... | collective-permute-start | bytes 12344 | tf_op jit(solution)/shard_map/ppermute | solution.py:27
  416.0 4.4 %collective-permute-start.15 = (f32[2,514,1]{1,0,2:T(2,128)S(1)}, f32[2,514,1]{1,0,2:T(2,128)S(1)}, u32[]{:S(2)}, u32[]{:S(2)}) collective-permute-start(f32[2,514,1]{1,0,2:T(2,128)S(1)} %copy.26), channel_id=1, source_target_pairs={{0,1},{1,2},{2,3},{4,5},{5,6},{6,7},{8,9},{9,10},{10,11},{12,13},{... | collective-permute-start | bytes 12344 | tf_op jit(solution)/shard_map/ppermute | solution.py:25
  421.4 4.9 %copy-start.5 = (f32[2,512,1024]{2,1,0:T(8,128)S(1)}, f32[2,512,1024]{2,1,0:T(8,128)}, u32[]{:S(2)}) copy-start(f32[2,512,1024]{2,1,0:T(8,128)} %copy-done.4) | copy-start | bytes 12582916

commit v2 on v1

--- a/solution.py
+++ b/solution.py
@@ -365,7 +365,11 @@
             )
 
 
-def prior(q):
+def cost(flops, moved):
+    return pl.CostEstimate(flops=int(flops), bytes_accessed=int(moved), transcendentals=0)
+
+
+def prior(q, make_fields):
     across, along = lax.axis_size("gx"), lax.axis_size("gy")
     nvec, bx, by = q.shape
     length = by * along
@@ -375,64 +379,154 @@
     mats, wave = line_tables(length)
     fhi, flo = two_parts(mats)
     thi, tlo = two_parts(np.swapaxes(mats, 1, 2))
-    params = pltpu.CompilerParams(vmem_limit_bytes=58 * 2**20)
-    table = pl.BlockSpec(fhi.shape, lambda v: (0, 0, 0))
-    lines = pl.BlockSpec((along, 1, rows, by), lambda v: (0, v, 0, 0))
-    packed = pl.BlockSpec((count, 1, rows, width), lambda v: (0, v, 0, 0))
-    lines_shape = jax.ShapeDtypeStruct((along, nvec, rows, by), jnp.float32)
-    packed_shape = jax.ShapeDtypeStruct((count, nvec, rows, width), jnp.float32)
-
-    send = jnp.swapaxes(q.reshape(nvec, along, rows, by), 0, 1)
-    whole_y = lax.all_to_all(send, "gy", 0, 0, tiled=True)
-    spec_y = pl.pallas_call(
-        y_forward, grid=(nvec,), in_specs=[lines, table, table], out_specs=packed,
-        out_shape=packed_shape, compiler_params=params, name="y_forward",
-    )(whole_y, fhi, flo)
-    whole_x = lax.all_to_all(spec_y, ("gx", "gy"), 0, 0, tiled=True)
+    params = pltpu.CompilerParams(vmem_limit_bytes=VMEM_BYTES)
+    lines_shape = jax.ShapeDtypeStruct((along, 1, rows, by), jnp.float32)
+    packed_shape = jax.ShapeDtypeStruct((count, 1, rows, width), jnp.float32)
+    work = 6 * mats.size * bx * by // length
+    moved = 8 * bx * by + 4 * mats.size
+
     me = lax.axis_index("gx") * along + lax.axis_index("gy")
     ky = lax.dynamic_slice_in_dim(
         jnp.asarray(wave.reshape(1, length), jnp.float32), me * width, width, axis=1
     )
     kx = jnp.asarray(wave[:, :, None], jnp.float32)
-    done_x = pl.pallas_call(
-        x_apply, out_shape=packed_shape, compiler_params=params, name="x_apply",
-    )(whole_x, ky, kx, thi, tlo, fhi, flo)
-    back_y = lax.all_to_all(done_x, ("gx", "gy"), 0, 0, tiled=True)
-    done_y = pl.pallas_call(
-        y_inverse, grid=(nvec,), in_specs=[packed, table, table], out_specs=lines,
-        out_shape=lines_shape, compiler_params=params, name="y_inverse",
-    )(back_y, thi, tlo)
-    back = lax.all_to_all(done_y, "gy", 0, 0, tiled=True)
-    return jnp.swapaxes(back, 0, 1).reshape(nvec, bx, by)
-
-
-def data_term(flux_perturbation, archived_nominal_heat_levels, archived_solidity_labels):
-    capacity = jnp.where(
-        archived_solidity_labels == 0, 1.0, jnp.where(archived_solidity_labels == 1, 4.0, 1.25)
-    ).astype(jnp.float32)
-    diffusion_advance = jnp.where(
-        archived_solidity_labels == 0, 1.0, jnp.where(archived_solidity_labels == 1, 0.6, 0.35)
-    ).astype(jnp.float32)
-    diffusion_advance = diffusion_advance * (1.0 + 0.5 * jnp.tanh(archived_nominal_heat_levels))
-    first_u = TIME_STEP * flux_perturbation / capacity[0, 0]
-    second_top = TIME_STEP * flux_perturbation + TIME_STEP * (
-        diffusion_advance[0, 0] * (surface_rim(first_u) - 6.0 * first_u) + flux_perturbation
-    )
-    second_low = TIME_STEP * diffusion_advance[0, 1] * first_u
-    top_u = second_top / capacity[1, 0]
-    low_u = second_low / capacity[1, 1]
-    third_top = second_top + TIME_STEP * (
-        diffusion_advance[1, 0] * (surface_rim(top_u) - 6.0 * top_u + low_u) + flux_perturbation
-    )
-    misfit = OBS_WEIGHT * third_top / capacity[1, 0]
-    adj_three = misfit / capacity[1, 0]
-    push_top = TIME_STEP * diffusion_advance[1, 0] * adj_three
-    adj_two_top = adj_three + (surface_rim(push_top) - 6.0 * push_top) / capacity[1, 0]
-    adj_two_low = push_top / capacity[1, 1]
-    pull_top = TIME_STEP * diffusion_advance[0, 0] * adj_two_top
-    pull_low = TIME_STEP * diffusion_advance[0, 1] * adj_two_low
-    adj_one_top = adj_two_top + (surface_rim(pull_top) - 6.0 * pull_top + pull_low) / capacity[0, 0]
-    return TIME_STEP * (adj_three + adj_two_top + adj_one_top)
+    turns = range(nvec)
+    whole_y = [
+        lax.all_to_all(q[v].reshape(along, 1, rows, by), "gy", 0, 0, tiled=True) for v in turns
+    ]
+    spec_y = [
+        pl.pallas_call(
+            y_forward, out_shape=packed_shape, compiler_params=params, name="y_forward",
+            cost_estimate=cost(work, moved),
+        )(whole_y[v], fhi, flo)
+        for v in turns
+    ]
+    spec_y[-1], fields = lax.optimization_barrier((spec_y[-1], make_fields()))
+    whole_x = [lax.all_to_all(spec_y[v], ("gx", "gy"), 0, 0, tiled=True) for v in turns]
+    done_x = [
+        pl.pallas_call(
+            x_apply, out_shape=packed_shape, compiler_params=params, name="x_apply",
+            cost_estimate=cost(4 * work, 2 * moved),
+        )(whole_x[v], ky, kx, thi, tlo, fhi, flo)
+        for v in turns
+    ]
+    done_x[-1], fields = lax.optimization_barrier((done_x[-1], fields))
+    data = data_part(fields, q)
+    back_y = [lax.all_to_all(done_x[v], ("gx", "gy"), 0, 0, tiled=True) for v in turns]
+    back_y[-1], data = lax.optimization_barrier((back_y[-1], data))
+    done_y = [
+        pl.pallas_call(
+            y_inverse, out_shape=lines_shape, compiler_params=params, name="y_inverse",
+            cost_estimate=cost(work, moved),
+        )(back_y[v], thi, tlo)
+        for v in turns
+    ]
+    back = [lax.all_to_all(done_y[v], "gy", 0, 0, tiled=True) for v in turns]
+    return [back[v].reshape(bx, by) for v in turns], data
+
+
+RIM = 8
+VMEM_BYTES = 58 * 2**20
+
+
+def shift(axis, step):
+    count = lax.axis_size(axis)
+    return [(i, i + step) for i in range(count) if 0 <= i + step < count]
+
+
+def rims(q, heat, labels):
+    bx, by = q.shape[1:]
+    near = lambda cut: jnp.concatenate(
+        [
+            cut(q),
+            (cut(labels) + 1).astype(jnp.float32).reshape((-1,) + cut(q).shape[1:]),
+            cut(heat).reshape((-1,) + cut(q).shape[1:])[:-1],
+        ]
+    )
+    above = lax.ppermute(near(lambda f: f[..., bx - RIM :, :]), "gx", shift("gx", 1))
+    below = lax.ppermute(near(lambda f: f[..., :RIM, :]), "gx", shift("gx", -1))
+    ends = []
+    for cols, step in ((slice(0, RIM), -1), (slice(by - RIM, by), 1)):
+        line = jnp.concatenate(
+            [above[..., cols], near(lambda f: f[..., cols]), below[..., cols]], axis=1
+        )
+        line = lax.ppermute(jnp.swapaxes(line, 1, 2), "gy", shift("gy", step))
+        ends.append(jnp.swapaxes(line, 1, 2))
+    return above, below, ends[0], ends[1]
+
+
+def widened(q, heat, labels, above, below, after, before):
+    main = jnp.concatenate(
+        [
+            q,
+            (labels + 1).astype(jnp.float32).reshape((-1,) + q.shape[1:]),
+            heat.reshape((-1,) + q.shape[1:])[:-1],
+        ]
+    )
+    tall = jnp.concatenate([above, main, below], axis=1)
+    gap = jnp.zeros(tall.shape[:2] + (128 - 2 * RIM,), jnp.float32)
+    return jnp.concatenate([tall, after, gap, before], axis=2)
+
+
+def data_strips(f_ref, out_ref):
+    nvec, bx, by = out_ref.shape
+    strip = 32
+    tall, wide = strip + 2 * RIM, f_ref.shape[2]
+
+    def rim(f):
+        return (pltpu.roll(f, 1, 0) + pltpu.roll(f, tall - 1, 0)) + (
+            pltpu.roll(f, 1, 1) + pltpu.roll(f, wide - 1, 1)
+        )
+
+    def one(s, carry):
+        first = pl.multiple_of(s * strip, strip)
+        field = lambda i: f_ref[i, pl.ds(first, tall), :]
+
+        def inverse_capacity(label):
+            return jnp.where(label == 2.0, 0.25, jnp.where(label == 3.0, 0.8, 1.0))
+
+        def conduct(label, level):
+            base = jnp.where(
+                label == 1.0, 1.0, jnp.where(label == 2.0, 0.6, jnp.where(label == 3.0, 0.35, 0.0))
+            )
+            return TIME_STEP * base * (1.0 + 0.5 * jnp.tanh(level))
+
+        label = [field(nvec + i) for i in range(4)]
+        ic_top0, ic_top1 = inverse_capacity(label[0]), inverse_capacity(label[2])
+        ic_low1 = inverse_capacity(label[3])
+        c_top0 = conduct(label[0], field(nvec + 4))
+        c_low0 = conduct(label[1], field(nvec + 5))
+        c_top1 = conduct(label[2], field(nvec + 6))
+        for v in range(nvec):
+            q = field(v)
+            first_u = TIME_STEP * q * ic_top0
+            second_top = (2.0 * TIME_STEP) * q + c_top0 * (rim(first_u) - 6.0 * first_u)
+            top_u = second_top * ic_top1
+            low_u = c_low0 * first_u * ic_low1
+            third_top = (
+                second_top + c_top1 * (rim(top_u) - 6.0 * top_u + low_u) + TIME_STEP * q
+            )
+            adj_three = OBS_WEIGHT * third_top * ic_top1 * ic_top1
+            push_top = c_top1 * adj_three
+            adj_two = adj_three + (rim(push_top) - 6.0 * push_top) * ic_top1
+            pull_top = c_top0 * adj_two
+            pull_low = c_low0 * (push_top * ic_low1)
+            adj_one = adj_two + (rim(pull_top) - 6.0 * pull_top + pull_low) * ic_top0
+            total = TIME_STEP * (adj_three + adj_two + adj_one)
+            out_ref[v, pl.ds(first, strip), :] = total[RIM : RIM + strip, :by]
+        return carry
+
+    lax.fori_loop(0, bx // strip, one, 0)
+
+
+def data_part(fields, like):
+    return pl.pallas_call(
+        data_strips,
+        out_shape=jax.ShapeDtypeStruct(like.shape, jnp.float32),
+        compiler_params=pltpu.CompilerParams(vmem_limit_bytes=VMEM_BYTES),
+        cost_estimate=cost(400 * like.size, 4 * fields.size + 4 * like.size),
+        name="data_strips",
+    )(fields)
 
 
 def shards(q, heat, labels):
@@ -440,9 +534,11 @@
     along, across = lax.axis_size("gy"), lax.axis_size("gx")
     rows, width = bx // along, by // across
     square = bx * across == by * along
-    if not square or rows % 16 or width % 128 or by % (by * along // OUTER):
+    if not square or rows % 16 or width % 128 or by % (by * along // OUTER) or bx % 32:
         return shards_general(q, heat, labels)
-    return data_term(q, heat, labels) + prior(q)
+    q, *beyond = lax.optimization_barrier((q, *rims(q, heat, labels)))
+    parts, data = prior(q, lambda: widened(q, heat, labels, *beyond))
+    return jnp.stack([data[v] + part for v, part in enumerate(parts)])
 
 
 def solution(mesh):

time: 442 us -> 411 us (0.930)
  other arithmetic: 94.2 us -> 23 us
  Pallas kernels: 37.5 us -> 96.6 us
  local copies, waits for them, and re-layouts: 22.4 us -> 57.5 us
  blocking collectives: 51.2 us -> 26.3 us
  starting transfers between devices: 67.4 us -> 49.5 us
  waiting for transfers between devices: 166 us -> 152 us
    ppermute x16 -> x4, waiting for transfers between devices: 76.3 us -> 4.24 us  [the longest x2 4.23 us: rims(): line = lax.ppermute(jnp.swapaxes(line, 1, 2), 'gy', shift('gy', step))]
    mul x5 -> x0, other arithmetic: 60.4 us -> none  [the longest x2 31 us: data_term(): push_top = TIME_STEP * diffusion_advance[1, 0] * adj_three]
    all_to_all x3 -> x7, waiting for transfers between devices: 89.6 us -> 148 us  [the longest x2 69.6 us: prior(): lax.all_to_all(spec_y[v], ('gx', 'gy'), 0, 0, tiled=True)]
    pallas_call x2 -> x5, Pallas kernels: 19.1 us -> 64.1 us  [the longest x1 34 us: data_part(): pl.pallas_call(data_strips, out_shape=jax.ShapeDtypeStruct(like.shape, jn...]
    ppermute x16 -> x4, starting transfers between devices: 49.7 us -> 12.3 us  [the longest x2 6.16 us: rims(): line = lax.ppermute(jnp.swapaxes(line, 1, 2), 'gy', shift('gy', step))]
    all_to_all x1, blocking collectives: 51.2 us -> 26.3 us  [prior(): lax.all_to_all(q[v].reshape(along, 1, rows, by), 'gy', 0, 0, tiled=True)]
    concatenate x0 -> x1, local copies, waits for them, and re-layouts: none -> 24.7 us  [widened(): return jnp.concatenate([tall, after, gap, before], axis=2)]
    all_to_all x3 -> x7, starting transfers between devices: 17.7 us -> 37.2 us  [the longest x2 11.5 us: prior(): lax.all_to_all(spec_y[v], ('gx', 'gy'), 0, 0, tiled=True)]
  transfers between devices with their start and end apart: 19 -> 11, of which waited for: 6 -> 8; matrix products, arithmetic and copies ran while one was open for 21% -> 15% of each run, Pallas kernels for 0% -> 24%
where the time goes in v2:
time: 411 us; the launch traced here: 405 us
  waiting for transfers between devices  152 us (37%)
  Pallas kernels  96.6 us (24%)
  local copies, waits for them, and re-layouts  57.5 us (14%)
  starting transfers between devices  49.5 us (12%)
  blocking collectives  26.3 us (6%)
  other arithmetic  23 us (6%)
    all_to_all x2, waiting for transfers between devices, prior(): lax.all_to_all(spec_y[v], ('gx', 'gy'), 0, 0, tiled=True)  69.6 us
    all_to_all x2, waiting for transfers between devices, prior(): back = [lax.all_to_all(done_y[v], 'gy', 0, 0, tiled=True) for v in turns]  41.3 us
    all_to_all x2, waiting for transfers between devices, prior(): lax.all_to_all(done_x[v], ('gx', 'gy'), 0, 0, tiled=True)  36.8 us
    pallas_call x1, Pallas kernels, data_part(): pl.pallas_call(data_strips, out_shape=jax.ShapeDtypeStruct(like.shape, jn...  34 us
    pallas_call x2, Pallas kernels, prior(): pl.pallas_call(x_apply, out_shape=packed_shape, compiler_params=params, n...  32.5 us
    all_to_all x1, blocking collectives, prior(): lax.all_to_all(q[v].reshape(along, 1, rows, by), 'gy', 0, 0, tiled=True)  26.3 us
    concatenate x1, local copies, waits for them, and re-layouts, widened(): return jnp.concatenate([tall, after, gap, before], axis=2)  24.7 us
    pallas_call x2, Pallas kernels, prior(): pl.pallas_call(y_forward, out_shape=packed_shape, compiler_params=params,...  15.1 us
  transfers between devices with their start and end apart: 11, of which 8 were waited for; matrix products, arithmetic and copies ran while one was open for 15% of the time, Pallas kernels for 24%

profile of v2, /device:TPU:17, one launch (start us, length us, event | category | flops | bytes accessed | tf_op | source)
XLA Modules:
  0.0 405.1 jit_solution(11807430284151156500)
XLA Ops:
  0.0 1.0 fusion.2
  1.0 1.0 add_convert_fusion.1
  2.0 0.9 fusion.5
  2.9 0.7 pad_maximum_fusion.2
  3.6 3.1 collective-permute-start
  6.8 0.7 pad_maximum_fusion.3
  7.5 3.0 collective-permute-start.1
  10.5 2.9 fusion
  13.4 1.9 fusion.1
  15.3 2.4 fusion.4
  17.7 2.1 copy.37
  19.8 0.8 add_convert_fusion.3
  20.7 0.9 copy.35
  21.6 0.8 add_convert_fusion.4
  22.4 0.3 copy.30
  22.7 1.2 copy.36
  24.0 0.3 copy.24
  24.3 1.2 copy.34
  25.5 0.1 fusion.6
  25.6 0.1 copy.31
  25.6 0.9 fusion.7
  26.5 0.1 copy.32
  26.6 0.1 maximum_bitcast_fusion.1
  26.7 4.2 %collective-permute-start.3 = (f32[9,8,528]{2,1,0:T(8,128)S(1)}, f32[9,8,528]{2,1,0:T(8,128)S(1)}, u32[]{:S(2)}, u32[]{:S(2)}) collective-permute-start(f32[9,8,528]{2,1,0:T(8,128)S(1)} %maximum_bitcast_fusion.1), channel_id=1, source_target_pairs={{0,1},{1,2},{2,3},{4,5},{5,6},{6,7},{8,9},{9,10},{10,11},{12,13},{... | collective-permute-start | bytes 456200 | tf_op jit(solution)/shard_map/ppermute | solution.py:453
  31.0 0.1 copy.25
  31.0 0.1 copy.26
  31.1 0.1 maximum_bitcast_fusion
  31.3 1.9 collective-permute-start.2
  33.2 0.3 collective-permute-done.3
  33.4 0.7 copy.33
  34.1 4.0 collective-permute-done.2
  38.1 2.1 copy.27
  40.2 4.0 fusion.3
  44.3 26.3 %all_to_all.40.x_ref = f32[4,1,128,1024]{3,2,1,0:T(8,128)} all-to-all(f32[4,1,128,1024]{3,2,1,0:T(8,128)S(1)} %bitcast.26), channel_id=1, replica_groups=mesh['gx'=8,'gy'=4] {'gy'}, dimensions={0} | all-to-all | bytes 4194304 | tf_op jit(solution)/shard_map/all_to_all | solution.py:395
  70.6 5.4 %all-to-all-start.3 = ((f32[4,1,128,1024]{3,2,1,0:T(8,128)}), f32[4,1,128,1024]{3,2,1,0:T(8,128)}, u32[]{:S(2)}, u32[]{:S(2)}) async-start(f32[4,1,128,1024]{3,2,1,0:T(8,128)} %bitcast.25), calls=%async_computation.3 | async-start | bytes 4194304 | tf_op jit(solution)/shard_map/all_to_all | solution.py:395
  76.0 4.4 %add_convert_fusion = f32[2,2,512,1024]{3,2,1,0:T(8,128)S(1)} fusion(s32[2,2,512,1024]{3,2,1,0:T(8,128)} %param.11), kind=kLoop, calls=%fused_computation.1 | loop fusion | flops 4194304 | bytes 16777216 | tf_op jit(solution)/shard_map/convert_element_type | solution.py:462
  80.5 3.5 slice.108
  84.0 0.5 copy-done
  84.4 8.2 %pad_maximum_fusion = f32[9,528,1024]{2,1,0:T(8,128)} fusion(f32[9,8,1024]{2,1,0:T(8,128)} %collective-permute-done.1, f32[3,512,1024]{2,1,0:T(8,128)S(1)} %slice.108, f32[4,512,1024]{2,1,0:T(8,128)S(1)} %bitcast.20, f32[2,512,1024]{2,1,0:T(8,128)S(1)} %copy-done, f32[9,8,1024]{2,1,0:T(8,128)S(1)} %collective-permute-done), kind=kLoop, calls=%fused_computation | loop fusion | flops 19464192 | bytes 38928384 | tf_op jit(solution)/shard_map/concatenate | solution.py:466
  92.6 1.6 broadcast_in_dim.3
  94.2 24.7 %concatenate.35.f_ref = f32[9,528,1152]{2,1,0:T(8,128)} concatenate(f32[9,528,1024]{2,1,0:T(8,128)} %pad_maximum_fusion, f32[9,528,8]{2,1,0:T(8,128)} %bitcast.22, f32[9,528,112]{2,1,0:T(8,128)} %broadcast_in_dim.3, f32[9,528,8]{2,1,0:T(8,128)S(1)} %bitcast.21), dimensions={2} | concatenate | bytes 43794432 | tf_op jit(solution)/shard_map/concatenate | solution.py:468
  118.9 7.6 %y_forward.2 = f32[32,1,128,128]{3,2,1,0:T(8,128)} custom-call(f32[4,1,128,1024]{3,2,1,0:T(8,128)} %all_to_all.40.x_ref, bf16[8,512,512]{2,1,0:T(8,128)(2,1)} %constant.37.clone.hi_ref.ihi_ref, bf16[8,512,512]{2,1,0:T(8,128)(2,1)} %constant.38.clone.lo_ref.ilo_ref), custom_call_target="tpu_custom_call" | custom-call | flops 1610612736 | bytes 12582912 | tf_op jit(solution)/shard_map/y_forward/pallas_call | solution.py:398
  126.5 5.9 %all-to-all-start.1 = ((f32[32,1,128,128]{3,2,1,0:T(8,128)}), f32[32,1,128,128]{3,2,1,0:T(8,128)S(1)}, u32[]{:S(2)}, u32[]{:S(2)}) async-start(f32[32,1,128,128]{3,2,1,0:T(8,128)} %y_forward.2), calls=%async_computation.1 | async-start | bytes 4194304 | tf_op jit(solution)/shard_map/all_to_all | solution.py:405
  132.4 7.5 %y_forward.3 = f32[32,1,128,128]{3,2,1,0:T(8,128)} custom-call(f32[4,1,128,1024]{3,2,1,0:T(8,128)} %all-to-all-done.3.x_ref, bf16[8,512,512]{2,1,0:T(8,128)(2,1)} %constant.37.clone.hi_ref.ihi_ref, bf16[8,512,512]{2,1,0:T(8,128)(2,1)} %constant.38.clone.lo_ref.ilo_ref), custom_call_target="tpu_custom_call" | custom-call | flops 1610612736 | bytes 12582912 | tf_op jit(solution)/shard_map/y_forward/pallas_call | solution.py:398
  139.9 39.8 %all-to-all-done.1.x_ref = f32[32,1,128,128]{3,2,1,0:T(8,128)S(1)} async-done(((f32[32,1,128,128]{3,2,1,0:T(8,128)}), f32[32,1,128,128]{3,2,1,0:T(8,128)S(1)}, u32[]{:S(2)}, u32[]{:S(2)}) %all-to-all-start.1) | async-done | bytes 2097184 | tf_op jit(solution)/shard_map/all_to_all | solution.py:405
  179.7 1.4 copy-done.3
  181.1 5.6 %all-to-all-start.4 = ((f32[32,1,128,128]{3,2,1,0:T(8,128)}), f32[32,1,128,128]{3,2,1,0:T(8,128)S(1)}, u32[]{:S(2)}, u32[]{:S(2)}) async-start(f32[32,1,128,128]{3,2,1,0:T(8,128)} %y_forward.3), calls=%async_computation.4 | async-start | bytes 4194304 | tf_op jit(solution)/shard_map/all_to_all | solution.py:405
  186.8 1.2 constant_dynamic-slice_fusion.ky_ref
  188.0 16.3 %x_apply.2 = f32[32,1,128,128]{3,2,1,0:T(8,128)} custom-call(f32[32,1,128,128]{3,2,1,0:T(8,128)} %copy-done.3, f32[1,128]{1,0:T(1,128)} %constant_dynamic-slice_fusion.ky_ref, f32[8,512,1]{2,1,0:T(8,128)} %constant.36.clone.kx_ref, bf16[8,512,512]{2,1,0:T(8,128)(2,1)} %constant.39.clone.fhi_ref.hi_ref, bf16[8,512,512]{2,1,0:T(8,128)(2,1)} %constant.40.clone.flo_ref.lo_ref, ...), custom_call_target="tpu_custom_call" | custom-call | flops 6442450944 | bytes 25165824 | tf_op jit(solution)/shard_map/x_apply/pallas_call | solution.py:407
  204.3 29.8 %all-to-all-done.4.x_ref = f32[32,1,128,128]{3,2,1,0:T(8,128)S(1)} async-done(((f32[32,1,128,128]{3,2,1,0:T(8,128)}), f32[32,1,128,128]{3,2,1,0:T(8,128)S(1)}, u32[]{:S(2)}, u32[]{:S(2)}) %all-to-all-start.4) | async-done | bytes 2097184 | tf_op jit(solution)/shard_map/all_to_all | solution.py:405
  234.1 1.3 copy-done.2
  235.4 5.6 %all-to-all-start.2 = ((f32[32,1,128,128]{3,2,1,0:T(8,128)}), f32[32,1,128,128]{3,2,1,0:T(8,128)S(1)}, u32[]{:S(2)}, u32[]{:S(2)}) async-start(f32[32,1,128,128]{3,2,1,0:T(8,128)} %x_apply.2), calls=%async_computation.2 | async-start | bytes 4194304 | tf_op jit(solution)/shard_map/all_to_all | solution.py:415
  241.0 16.3 %x_apply.3 = f32[32,1,128,128]{3,2,1,0:T(8,128)} custom-call(f32[32,1,128,128]{3,2,1,0:T(8,128)} %copy-done.2, f32[1,128]{1,0:T(1,128)} %constant_dynamic-slice_fusion.ky_ref, f32[8,512,1]{2,1,0:T(8,128)} %constant.36.clone.kx_ref, bf16[8,512,512]{2,1,0:T(8,128)(2,1)} %constant.39.clone.fhi_ref.hi_ref, bf16[8,512,512]{2,1,0:T(8,128)(2,1)} %constant.40.clone.flo_ref.lo_ref, ...), custom_call_target="tpu_custom_call" | custom-call | flops 6442450944 | bytes 25165824 | tf_op jit(solution)/shard_map/x_apply/pallas_call | solution.py:407
  257.3 31.0 %all-to-all-done.2.x_ref = f32[32,1,128,128]{3,2,1,0:T(8,128)S(1)} async-done(((f32[32,1,128,128]{3,2,1,0:T(8,128)}), f32[32,1,128,128]{3,2,1,0:T(8,128)S(1)}, u32[]{:S(2)}, u32[]{:S(2)}) %all-to-all-start.2) | async-done | bytes 2097184 | tf_op jit(solution)/shard_map/all_to_all | solution.py:415
  288.3 5.7 %all-to-all-start.5 = ((f32[32,1,128,128]{3,2,1,0:T(8,128)}), f32[32,1,128,128]{3,2,1,0:T(8,128)}, u32[]{:S(2)}, u32[]{:S(2)}) async-start(f32[32,1,128,128]{3,2,1,0:T(8,128)} %x_apply.3), calls=%async_computation.5 | async-start | bytes 4194304 | tf_op jit(solution)/shard_map/all_to_all | solution.py:415
  294.0 34.0 %data_strips.1 = f32[2,512,1024]{2,1,0:T(8,128)} custom-call(f32[9,528,1152]{2,1,0:T(8,128)} %concatenate.35.f_ref), custom_call_target="tpu_custom_call" | custom-call | flops 419430400 | bytes 26091520 | tf_op jit(solution)/shard_map/data_strips/pallas_call | solution.py:523
  327.9 7.5 %y_inverse.3 = f32[4,1,128,1024]{3,2,1,0:T(8,128)} custom-call(f32[32,1,128,128]{3,2,1,0:T(8,128)} %copy-done.1, bf16[8,512,512]{2,1,0:T(8,128)(2,1)} %constant.39.clone.fhi_ref.hi_ref, bf16[8,512,512]{2,1,0:T(8,128)(2,1)} %constant.40.clone.flo_ref.lo_ref), custom_call_target="tpu_custom_call" | custom-call | flops 1610612736 | bytes 12582912 | tf_op jit(solution)/shard_map/y_inverse/pallas_call | solution.py:418
  335.5 5.8 %all-to-all-done.5.x_ref = f32[32,1,128,128]{3,2,1,0:T(8,128)} async-done(((f32[32,1,128,128]{3,2,1,0:T(8,128)}), f32[32,1,128,128]{3,2,1,0:T(8,128)}, u32[]{:S(2)}, u32[]{:S(2)}) %all-to-all-start.5) | async-done | bytes 2097184 | tf_op jit(solution)/shard_map/all_to_all | solution.py:415
  341.3 3.6 all-to-all-start.7
  344.9 7.5 %y_inverse.2 = f32[4,1,128,1024]{3,2,1,0:T(8,128)} custom-call(f32[32,1,128,128]{3,2,1,0:T(8,128)} %all-to-all-done.5.x_ref, bf16[8,512,512]{2,1,0:T(8,128)(2,1)} %constant.39.clone.fhi_ref.hi_ref, bf16[8,512,512]{2,1,0:T(8,128)(2,1)} %constant.40.clone.flo_ref.lo_ref), custom_call_target="tpu_custom_call" | custom-call | flops 1610612736 | bytes 12582912 | tf_op jit(solution)/shard_map/y_inverse/pallas_call | solution.py:418
  352.4 16.4 %all-to-all-done.7 = f32[4,1,128,1024]{3,2,1,0:T(8,128)S(1)} async-done(((f32[4,1,128,1024]{3,2,1,0:T(8,128)}), f32[4,1,128,1024]{3,2,1,0:T(8,128)S(1)}, u32[]{:S(2)}, u32[]{:S(2)}) %all-to-all-start.7) | async-done | bytes 2097184 | tf_op jit(solution)/shard_map/all_to_all | solution.py:424
  368.8 5.3 %all-to-all-start.6 = ((f32[4,1,128,1024]{3,2,1,0:T(8,128)}), f32[4,1,128,1024]{3,2,1,0:T(8,128)}, u32[]{:S(2)}, u32[]{:S(2)}) async-start(f32[4,1,128,1024]{3,2,1,0:T(8,128)} %y_inverse.2), calls=%async_computation.6 | async-start | bytes 4194304 | tf_op jit(solution)/shard_map/all_to_all | solution.py:424
  374.1 24.9 %all-to-all-done.6 = f32[4,1,128,1024]{3,2,1,0:T(8,128)} async-done(((f32[4,1,128,1024]{3,2,1,0:T(8,128)}), f32[4,1,128,1024]{3,2,1,0:T(8,128)}, u32[]{:S(2)}, u32[]{:S(2)}) %all-to-all-start.6) | async-done | bytes 2097184 | tf_op jit(solution)/shard_map/all_to_all | solution.py:424
  399.1 6.0 %slice_add_fusion.1 = (f32[2,512,1024]{2,1,0:T(8,128)}, f32[2,512,1024]{2,1,0:T(8,128)}) fusion(f32[1,512,1024]{2,1,0:T(8,128)} %bitcast.16, f32[2,512,1024]{2,1,0:T(8,128)} %data_strips.1, f32[1,512,1024]{2,1,0:T(8,128)S(1)} %bitcast.24, f32[2,512,1024]{2,1,0:T(8,128)} %custom-call), kind=kLoop, output_to_operand_aliasing={{0}: (3, {}), {1}: (3, {})}, calls=%fused_computation.4 | loop fusion | flops 1048576 | bytes 12582912 | tf_op jit(solution)/shard_map/add | solution.py:541
  (13 shorter events, 0.0 us)
Async XLA Ops:
  3.6 21.9 %collective-permute-start = (f32[9,8,1024]{2,1,0:T(8,128)}, f32[9,8,1024]{2,1,0:T(8,128)S(1)}, u32[]{:S(2)}, u32[]{:S(2)}) collective-permute-start(f32[9,8,1024]{2,1,0:T(8,128)} %pad_maximum_fusion.2), channel_id=1, source_target_pairs={{0,4},{4,8},{8,12},{12,16},{16,20},{20,24},{24,28},{1,5},{5,9},{9,... | collective-permute-start | bytes 884744 | tf_op jit(solution)/shard_map/ppermute | solution.py:446
  7.5 18.1 %collective-permute-start.1 = (f32[9,8,1024]{2,1,0:T(8,128)}, f32[9,8,1024]{2,1,0:T(8,128)}, u32[]{:S(2)}, u32[]{:S(2)}) collective-permute-start(f32[9,8,1024]{2,1,0:T(8,128)} %pad_maximum_fusion.3), channel_id=1, source_target_pairs={{4,0},{8,4},{12,8},{16,12},{20,16},{24,20},{28,24},{5,1},{9,5},{13... | collective-permute-start | bytes 884744 | tf_op jit(solution)/shard_map/ppermute | solution.py:447
  26.7 6.7 %collective-permute-start.3 = (f32[9,8,528]{2,1,0:T(8,128)S(1)}, f32[9,8,528]{2,1,0:T(8,128)S(1)}, u32[]{:S(2)}, u32[]{:S(2)}) collective-permute-start(f32[9,8,528]{2,1,0:T(8,128)S(1)} %maximum_bitcast_fusion.1), channel_id=1, source_target_pairs={{0,1},{1,2},{2,3},{4,5},{5,6},{6,7},{8,9},{9,10},{10,11},{12,13},{... | collective-permute-start | bytes 456200 | tf_op jit(solution)/shard_map/ppermute | solution.py:453
  31.3 6.9 %collective-permute-start.2 = (f32[9,8,528]{2,1,0:T(8,128)S(1)}, f32[9,8,528]{2,1,0:T(8,128)S(1)}, u32[]{:S(2)}, u32[]{:S(2)}) collective-permute-start(f32[9,8,528]{2,1,0:T(8,128)S(1)} %maximum_bitcast_fusion), channel_id=1, source_target_pairs={{1,0},{2,1},{3,2},{5,4},{6,5},{7,6},{9,8},{10,9},{11,10},{13,12},{... | collective-permute-start | bytes 456200 | tf_op jit(solution)/shard_map/ppermute | solution.py:453
  70.6 55.9 %all-to-all-start.3 = ((f32[4,1,128,1024]{3,2,1,0:T(8,128)}), f32[4,1,128,1024]{3,2,1,0:T(8,128)}, u32[]{:S(2)}, u32[]{:S(2)}) async-start(f32[4,1,128,1024]{3,2,1,0:T(8,128)} %bitcast.25), calls=%async_computation.3 | async-start | bytes 4194304 | tf_op jit(solution)/shard_map/all_to_all | solution.py:395
  80.4 4.0 copy-start
  126.5 53.2 %all-to-all-start.1 = ((f32[32,1,128,128]{3,2,1,0:T(8,128)}), f32[32,1,128,128]{3,2,1,0:T(8,128)S(1)}, u32[]{:S(2)}, u32[]{:S(2)}) async-start(f32[32,1,128,128]{3,2,1,0:T(8,128)} %y_forward.2), calls=%async_computation.1 | async-start | bytes 4194304 | tf_op jit(solution)/shard_map/all_to_all | solution.py:405
  179.7 1.4 copy-start.3
  181.1 52.9 %all-to-all-start.4 = ((f32[32,1,128,128]{3,2,1,0:T(8,128)}), f32[32,1,128,128]{3,2,1,0:T(8,128)S(1)}, u32[]{:S(2)}, u32[]{:S(2)}) async-start(f32[32,1,128,128]{3,2,1,0:T(8,128)} %y_forward.3), calls=%async_computation.4 | async-start | bytes 4194304 | tf_op jit(solution)/shard_map/all_to_all | solution.py:405
  234.0 1.3 copy-start.2
  235.4 52.9 %all-to-all-start.2 = ((f32[32,1,128,128]{3,2,1,0:T(8,128)}), f32[32,1,128,128]{3,2,1,0:T(8,128)S(1)}, u32[]{:S(2)}, u32[]{:S(2)}) async-start(f32[32,1,128,128]{3,2,1,0:T(8,128)} %x_apply.2), calls=%async_computation.2 | async-start | bytes 4194304 | tf_op jit(solution)/shard_map/all_to_all | solution.py:415
  288.3 39.7 %copy-start.1 = (f32[32,1,128,128]{3,2,1,0:T(8,128)}, f32[32,1,128,128]{3,2,1,0:T(8,128)S(1)}, u32[]{:S(2)}) copy-start(f32[32,1,128,128]{3,2,1,0:T(8,128)S(1)} %all-to-all-done.2.x_ref) | copy-start | bytes 6291460
  288.3 53.0 %all-to-all-start.5 = ((f32[32,1,128,128]{3,2,1,0:T(8,128)}), f32[32,1,128,128]{3,2,1,0:T(8,128)}, u32[]{:S(2)}, u32[]{:S(2)}) async-start(f32[32,1,128,128]{3,2,1,0:T(8,128)} %x_apply.3), calls=%async_computation.5 | async-start | bytes 4194304 | tf_op jit(solution)/shard_map/all_to_all | solution.py:415
  341.3 27.5 %all-to-all-start.7 = ((f32[4,1,128,1024]{3,2,1,0:T(8,128)}), f32[4,1,128,1024]{3,2,1,0:T(8,128)S(1)}, u32[]{:S(2)}, u32[]{:S(2)}) async-start(f32[4,1,128,1024]{3,2,1,0:T(8,128)} %y_inverse.3), calls=%async_computation.7 | async-start | bytes 4194304 | tf_op jit(solution)/shard_map/all_to_all | solution.py:424
  368.8 30.3 %all-to-all-start.6 = ((f32[4,1,128,1024]{3,2,1,0:T(8,128)}), f32[4,1,128,1024]{3,2,1,0:T(8,128)}, u32[]{:S(2)}, u32[]{:S(2)}) async-start(f32[4,1,128,1024]{3,2,1,0:T(8,128)} %y_inverse.2), calls=%async_computation.6 | async-start | bytes 4194304 | tf_op jit(solution)/shard_map/all_to_all | solution.py:424
